TPU v7x, 32 devices: a whole 2x2x4 slice. The times are simulated.
32 devices in a mesh: dp: 16 (over z, x, core), tensor: 2 (over y).
Axes of the slice: x: 2, y: 2, z: 4, core: 2. Of those that a mesh axis runs over, the one named last changes fastest.
Arguments:
- tokens: bfloat16 [4096, 768], P(('dp', 'tensor')), may hold values from -6 to 6
- ln1_gain: bfloat16 [768], P('dp'), may hold values from 0.099609375 to 1.8984375
- ln1_bias: bfloat16 [768], P('dp'), may hold values from -1.5 to 1.5
- ln2_gain: bfloat16 [768], P('dp'), may hold values from 0.099609375 to 1.8984375
- ln2_bias: bfloat16 [768], P('dp'), may hold values from -1.5 to 1.5
- w_qkv: bfloat16 [768, 2304], P('dp', 'tensor'), may hold values from -0.21875 to 0.21875
- w_out: bfloat16 [768, 768], P('tensor', 'dp'), may hold values from -0.875 to 0.875
- w_up: bfloat16 [768, 3072], P('dp', 'tensor'), may hold values from -0.21875 to 0.21875
- w_down: bfloat16 [3072, 768], P('tensor', 'dp'), may hold values from -0.109375 to 0.109375
- grad_out: bfloat16 [4096, 768], P(('dp', 'tensor')), may hold values from -6 to 6
- lengths: int32 [16, 4], P('dp'), may hold values from 1 to 192, 256 in all within a row
Outputs:
- output: bfloat16 [4096, 768], P(('dp', 'tensor'))
- grad_tokens: float32 [4096, 768], P(('dp', 'tensor'))
- grad_ln1_gain: float32 [768], P('dp')
- grad_ln1_bias: float32 [768], P('dp')
- grad_ln2_gain: float32 [768], P('dp')
- grad_ln2_bias: float32 [768], P('dp')
- grad_w_qkv: float32 [768, 2304], P('dp', 'tensor')
- grad_w_out: float32 [768, 768], P('tensor', 'dp')
- grad_w_up: float32 [768, 3072], P('dp', 'tensor')
- grad_w_down: float32 [3072, 768], P('tensor', 'dp')
Inputs may be any that keep to these rules, and one draw needn't show every extreme that they name: Each row of lengths gives, in order, the lengths of the 4 sequences packed into the 256 tokens of one group; a row sums to 256 and its longest sequence has exactly 192 tokens.
All inputs are finite; a program needn't handle non-finite values.
Results may differ from a plain program's by a relative error of at most 0.0099.
Values may be sent and summed in bfloat16 or wider, within the bound.
A program may use at most 128 MiB of HBM per device.

v0:
```python
import math

import jax
import jax.numpy as jnp
from jax import lax
from jax.sharding import PartitionSpec as P

HEAD = 64
ROT = 16


norm_eps = 1e-05
masked_score = -1e30


def layer_norm(values, norm_gain, norm_bias):
    center = values - jnp.mean(values, axis=-1, keepdims=True)
    spread = jnp.mean(center * center, axis=-1, keepdims=True)
    return center * lax.rsqrt(spread + norm_eps) * norm_gain + norm_bias


def norms_pair(rows_f, gain_one, bias_one, gain_two, bias_two):
    return (layer_norm(rows_f, gain_one, bias_one), layer_norm(rows_f, gain_two, bias_two))


def doc_layout(lengths_row, row_count):
    seq_ends = jnp.cumsum(lengths_row)
    starts = seq_ends - lengths_row
    places = jnp.arange(row_count, dtype=jnp.int32)
    segment = jnp.sum((places[:, None] >= seq_ends[None, :]).astype(jnp.int32), axis=1)
    chosen = segment[:, None] == jnp.arange(lengths_row.shape[0], dtype=jnp.int32)[None, :]
    seq_first = jnp.sum(jnp.where(chosen, starts[None, :], 0), axis=1)
    return (segment, places - seq_first, places)


def rope_tables(positions):
    frequency = jnp.arange(ROT // 2, dtype=jnp.float32)
    inverse = jnp.exp(frequency * (-2.0 * math.log(10000.0) / ROT))
    angles = positions.astype(jnp.float32)[:, None] * inverse[None, :]
    return (jnp.cos(angles), jnp.sin(angles))


def rotate(vectors, wave_cos, wave_sin):
    half_rot = ROT // 2
    first_half = vectors[..., :half_rot]
    second_half = vectors[..., half_rot:ROT]
    cos_heads = wave_cos[:, None, :]
    sin_heads = wave_sin[:, None, :]
    return jnp.concatenate(
        [
            first_half * cos_heads - second_half * sin_heads,
            second_half * cos_heads + first_half * sin_heads,
            vectors[..., ROT:],
        ],
        axis=-1,
    )


def contract(first_op, second_op, first_dim, second_dim):
    return lax.dot_general(
        first_op,
        second_op,
        (((first_dim,), (second_dim,)), ((), ())),
        preferred_element_type=jnp.float32,
    )


def per_device(
    tokens, ln1_gain, ln1_bias, ln2_gain, ln2_bias, w_qkv, w_out, w_up, w_down, grad_out, lengths
):
    tok_rows = tokens.shape[0]
    group_rows = tok_rows * lax.axis_size("tensor")
    local_heads = w_qkv.shape[1] // (3 * HEAD)
    score_scale = 1.0 / math.sqrt(HEAD)
    norm_params = jnp.stack([ln1_gain, ln1_bias, ln2_gain, ln2_bias], axis=0)
    qkv_full, up_full, out_full, down_full, norm_full = (
        lax.all_gather(w_qkv, "dp", axis=0, tiled=True),
        lax.all_gather(w_up, "dp", axis=0, tiled=True),
        lax.all_gather(w_out, "dp", axis=1, tiled=True),
        lax.all_gather(w_down, "dp", axis=1, tiled=True),
        lax.all_gather(norm_params, "dp", axis=1, tiled=True),
    )
    norm_float = norm_full.astype(jnp.float32)
    gain_one, bias_one, gain_two, bias_two = (
        norm_float[0],
        norm_float[1],
        norm_float[2],
        norm_float[3],
    )
    segment, positions, places = doc_layout(lengths[0], group_rows)
    wave_cos, wave_sin = rope_tables(positions)
    tokens_f = tokens.astype(jnp.float32)
    own_one, own_two = norms_pair(tokens_f, gain_one, bias_one, gain_two, bias_two)
    normed_one, normed_two = (
        lax.all_gather(own_one.astype(jnp.bfloat16), "tensor", axis=0, tiled=True),
        lax.all_gather(own_two.astype(jnp.bfloat16), "tensor", axis=0, tiled=True),
    )
    projected = jnp.dot(normed_one, qkv_full, preferred_element_type=jnp.float32).reshape(
        group_rows, local_heads, 3, HEAD
    )
    queries = rotate(projected[:, :, 0], wave_cos, wave_sin).astype(jnp.bfloat16)
    keys_all = rotate(projected[:, :, 1], wave_cos, wave_sin).astype(jnp.bfloat16)
    values_all = projected[:, :, 2].astype(jnp.bfloat16)
    block_rows = min(512, group_rows)
    block_count = group_rows // block_rows
    query_blocks = queries.reshape(block_count, block_rows, local_heads, HEAD)
    segment_blocks = segment.reshape(block_count, block_rows)
    place_blocks = places.reshape(block_count, block_rows)

    def block_scores(query_block, segment_block, place_block):
        scores = (
            jnp.einsum("qhd,khd->hqk", query_block, keys_all, preferred_element_type=jnp.float32)
            * score_scale
        )
        allowed = (segment_block[:, None] == segment[None, :]) & (
            place_block[:, None] >= places[None, :]
        )
        return jnp.where(allowed[None], scores, masked_score)

    def attend_block(block_items):
        query_block, segment_block, place_block = block_items
        scores = block_scores(query_block, segment_block, place_block)
        row_peak = jnp.max(scores, axis=-1, keepdims=True)
        exponent = jnp.exp(scores - row_peak)
        row_total = jnp.sum(exponent, axis=-1, keepdims=True)
        prob_low = (exponent / row_total).astype(jnp.bfloat16)
        attended_block = jnp.einsum(
            "hqk,khd->qhd", prob_low, values_all, preferred_element_type=jnp.float32
        )
        return (attended_block.astype(jnp.bfloat16), row_peak + jnp.log(row_total))

    attended_blocks, log_totals = lax.map(
        attend_block, (query_blocks, segment_blocks, place_blocks)
    )
    attended = attended_blocks.reshape(group_rows, local_heads * HEAD)
    hidden_pre = jnp.dot(normed_two, up_full, preferred_element_type=jnp.float32)
    activated = jax.nn.gelu(hidden_pre, approximate=False).astype(jnp.bfloat16)
    branch_terms = jnp.dot(attended, out_full, preferred_element_type=jnp.float32) + jnp.dot(
        activated, down_full, preferred_element_type=jnp.float32
    )
    branch_own = lax.psum_scatter(branch_terms, "tensor", scatter_dimension=0, tiled=True)
    output = (tokens_f + branch_own).astype(jnp.bfloat16)
    cotangent = lax.all_gather(grad_out, "tensor", axis=0, tiled=True)
    qkv_back, up_back, out_back, down_back = (
        lax.all_gather(w_qkv, "dp", axis=0, tiled=True),
        lax.all_gather(w_up, "dp", axis=0, tiled=True),
        lax.all_gather(w_out, "dp", axis=1, tiled=True),
        lax.all_gather(w_down, "dp", axis=1, tiled=True),
    )
    act_grad = contract(cotangent, down_back, 1, 1)
    gelu_value, gelu_pull = jax.vjp(
        lambda pre_act: jax.nn.gelu(pre_act, approximate=False), hidden_pre
    )
    pre_grad = gelu_pull(act_grad)[0].astype(jnp.bfloat16)
    grad_down_t = contract(cotangent, activated, 0, 0)
    grad_up = contract(normed_two, pre_grad, 0, 0)
    norm_two_grad = contract(pre_grad, up_back, 1, 1)
    att_grad = contract(cotangent, out_back, 1, 1).astype(jnp.bfloat16)
    grad_out_t = contract(cotangent, attended, 0, 0)
    att_blocks = att_grad.reshape(block_count, block_rows, local_heads, HEAD)

    def back_block(carry, block_items):
        key_grads, value_grads = carry
        query_block, segment_block, place_block, grad_block, log_block = block_items
        scores = block_scores(query_block, segment_block, place_block)
        probability = jnp.exp(scores - log_block)
        prob_grad = jnp.einsum(
            "qhd,khd->hqk", grad_block, values_all, preferred_element_type=jnp.float32
        )
        row_dot = jnp.sum(probability * prob_grad, axis=-1, keepdims=True)
        score_grad = (probability * (prob_grad - row_dot)).astype(jnp.bfloat16)
        query_grad = (
            jnp.einsum("hqk,khd->qhd", score_grad, keys_all, preferred_element_type=jnp.float32)
            * score_scale
        )
        key_grads = (
            key_grads
            + jnp.einsum(
                "hqk,qhd->khd", score_grad, query_block, preferred_element_type=jnp.float32
            )
            * score_scale
        )
        value_grads = value_grads + jnp.einsum(
            "hqk,qhd->khd",
            probability.astype(jnp.bfloat16),
            grad_block,
            preferred_element_type=jnp.float32,
        )
        return ((key_grads, value_grads), query_grad)

    zero_heads = jnp.zeros((group_rows, local_heads, HEAD), jnp.float32)
    (key_grads, value_grads), query_grads = lax.scan(
        back_block,
        (zero_heads, zero_heads),
        (query_blocks, segment_blocks, place_blocks, att_blocks, log_totals),
    )
    query_grads = query_grads.reshape(group_rows, local_heads, HEAD)
    proj_grad = (
        jnp.stack(
            [
                rotate(query_grads, wave_cos, -wave_sin),
                rotate(key_grads, wave_cos, -wave_sin),
                value_grads,
            ],
            axis=2,
        )
        .reshape(group_rows, 3 * local_heads * HEAD)
        .astype(jnp.bfloat16)
    )
    grad_qkv = contract(normed_one, proj_grad, 0, 0)
    norm_one_grad = contract(proj_grad, qkv_back, 1, 1)
    own_one_grad, own_two_grad = (
        lax.psum_scatter(norm_one_grad, "tensor", scatter_dimension=0, tiled=True),
        lax.psum_scatter(norm_two_grad, "tensor", scatter_dimension=0, tiled=True),
    )
    norm_value, norm_pull = jax.vjp(norms_pair, tokens_f, gain_one, bias_one, gain_two, bias_two)
    row_grad, gain_one_grad, bias_one_grad, gain_two_grad, bias_two_grad = norm_pull(
        (own_one_grad, own_two_grad)
    )
    grad_tokens = grad_out.astype(jnp.float32) + row_grad
    norm_grads = jnp.stack([gain_one_grad, bias_one_grad, gain_two_grad, bias_two_grad], axis=1)
    qkv_parts, up_parts, out_parts, down_parts, norm_parts = (
        lax.all_to_all(grad_qkv[None], "dp", split_axis=1, concat_axis=0, tiled=True),
        lax.all_to_all(grad_up[None], "dp", split_axis=1, concat_axis=0, tiled=True),
        lax.all_to_all(grad_out_t[None], "dp", split_axis=1, concat_axis=0, tiled=True),
        lax.all_to_all(grad_down_t[None], "dp", split_axis=1, concat_axis=0, tiled=True),
        lax.all_to_all(norm_grads[None], "dp", split_axis=1, concat_axis=0, tiled=True),
    )
    qkv_own = jnp.sum(qkv_parts, axis=0)
    up_own = jnp.sum(up_parts, axis=0)
    out_own = jnp.sum(out_parts, axis=0)
    down_own = jnp.sum(down_parts, axis=0)
    norm_own = jnp.sum(norm_parts, axis=0).T
    norm_total = lax.psum(norm_own, "tensor")
    return (
        output,
        grad_tokens,
        norm_total[0],
        norm_total[1],
        norm_total[2],
        norm_total[3],
        qkv_own,
        out_own.T,
        up_own,
        down_own.T,
    )


def solution(mesh):
    placed = (
        P(("dp", "tensor"), None),
        P("dp"),
        P("dp"),
        P("dp"),
        P("dp"),
        P("dp", "tensor"),
        P("tensor", "dp"),
        P("dp", "tensor"),
        P("tensor", "dp"),
        P(("dp", "tensor"), None),
        P("dp", None),
    )
    return jax.shard_map(
        per_device,
        mesh=mesh,
        in_specs=placed,
        out_specs=(
            P(("dp", "tensor"), None),
            P(("dp", "tensor"), None),
            P("dp"),
            P("dp"),
            P("dp"),
            P("dp"),
            P("dp", "tensor"),
            P("tensor", "dp"),
            P("dp", "tensor"),
            P("tensor", "dp"),
        ),
        check_vma=False,
    )
```

profile of v0, /device:TPU:8, one launch (start us, length us, event | category | flops | bytes accessed | tf_op | source)
XLA Modules:
  0.0 512.2 jit_solution(11290000425046274133)
XLA Ops:
  12.4 18.8 %all-gather = bf16[16,48,4]{1,2,0:T(4,128)(2,1)S(1)} all-gather(bf16[1,48,4]{1,2,0:T(4,128)(2,1)S(1)} %maximum_bitcast_fusion.3), channel_id=1, replica_groups=mesh['dp'=16,'tensor'=2] {'dp'}, dimensions={0}, use_global_device_ids=true | all-gather | bytes 6528 | tf_op jit(solution)/shard_map/all_gather | solution.py:81
  32.6 7.8 %all_gather.29 = bf16[256,768]{1,0:T(8,128)(2,1)S(1)} all-gather(bf16[128,768]{1,0:T(8,128)(2,1)S(1)} %get-tuple-element.112), channel_id=1, replica_groups=mesh['dp'=16,'tensor'=2] {'tensor'}, dimensions={0}, use_global_device_ids=true | all-gather | bytes 589824 | tf_op jit(solution)/shard_map/all_gather | solution.py:95
  40.7 7.1 %all_gather.35 = bf16[256,768]{1,0:T(8,128)(2,1)S(1)} all-gather(bf16[128,768]{1,0:T(8,128)(2,1)S(1)} %copy-done.17), channel_id=1, replica_groups=mesh['dp'=16,'tensor'=2] {'tensor'}, dimensions={0}, use_global_device_ids=true | all-gather | bytes 589824 | tf_op jit(solution)/shard_map/all_gather | solution.py:143
  47.8 19.8 %all_gather.31 = bf16[384,768]{0,1:T(8,128)(2,1)S(1)} all-gather(bf16[384,48]{0,1:T(8,128)(2,1)S(1)} %copy-done.20), channel_id=1, replica_groups=mesh['dp'=16,'tensor'=2] {'dp'}, dimensions={1}, use_global_device_ids=true | all-gather | bytes 626688 | tf_op jit(solution)/shard_map/all_gather | solution.py:79
  68.9 7.9 %all_gather.32 = bf16[256,768]{1,0:T(8,128)(2,1)} all-gather(bf16[128,768]{1,0:T(8,128)(2,1)S(1)} %get-tuple-element.113), channel_id=1, replica_groups=mesh['dp'=16,'tensor'=2] {'tensor'}, dimensions={0}, use_global_device_ids=true | all-gather | bytes 589824 | tf_op jit(solution)/shard_map/all_gather | solution.py:96
  77.2 2.3 fusion.49
  84.8 1.6 fusion.53
  86.5 8.5 %all-gather.7.cloned.1.call-done = bf16[768,1536]{1,0:T(8,128)(2,1)} async-done(((bf16[48,1536]{1,0:T(8,128)(2,1)}), bf16[768,1536]{1,0:T(8,128)(2,1)}) %all-gather.7.cloned.1.call-update) | async-done | bytes 2359312 | tf_op jit(solution)/shard_map/all_gather | solution.py:78
  95.0 2.6 fusion.50
  97.6 40.8 %all-gather.9.cloned.1.call-done = bf16[1536,768]{0,1:T(8,128)(2,1)} async-done(((bf16[1536,48]{0,1:T(8,128)(2,1)}), bf16[1536,768]{0,1:T(8,128)(2,1)}) %all-gather.9.cloned.1.call-update) | async-done | bytes 2359312 | tf_op jit(solution)/shard_map/all_gather | solution.py:80
  138.5 6.9 %add_convert_fusion = (bf16[256,1536]{1,0:T(8,128)(2,1)S(1)}, f32[256,1536]{1,0:T(8,128)}) fusion(f32[256,1536]{1,0:T(8,128)S(1)} %fusion.50, bf16[256,768]{1,0:T(8,128)(2,1)S(1)} %all_gather.35, bf16[1536,768]{0,1:T(8,128)(2,1)} %all-gather.9.cloned.1.call-done), kind=kOutput, calls=%fused_computation.8 | convolution fusion | flops 632291328 | bytes 6684672 | tf_op jit(solution)/shard_map/dot_general | solution.py:60
  146.3 1.7 fusion.52
  148.0 1.4 convolution_convert_fusion.2
  150.4 2.6 copy.120
  153.1 4.7 all-to-all-start.2
  157.9 19.2 %reduce-scatter.6.cloned.1.call-done = f32[128,768]{1,0:T(8,128)} async-done(((f32[256,768]{1,0:T(8,128)}), f32[128,768]{1,0:T(8,128)}) %reduce-scatter.6.cloned.1.call-update) | async-done | bytes 393232 | tf_op jit(solution)/shard_map/reduce_scatter | solution.py:214
  177.0 1.3 fusion.30
  178.5 2.1 fusion.27
  181.5 1.6 reduce.26
  184.8 5.7 %all-to-all-start = ((f32[16,1,192]{2,1,0:T(1,128)}), f32[16,1,192]{2,1,0:T(1,128)S(1)}, u32[]{:S(2)}, u32[]{:S(2)}) async-start(f32[16,1,192]{2,1,0:T(1,128)} %reshape.268), calls=%async_computation.3 | async-start | bytes 32768 | tf_op jit(solution)/shard_map/all_to_all | solution.py:227
  191.2 5.5 %copy.119 = f32[1,768,1152]{2,0,1:T(1,128)} copy(f32[1,768,1152]{2,1,0:T(8,128)S(1)} %convolution_bitcast_fusion.2) | data formatting | bytes 7077888 | tf_op jit(solution)/shard_map/broadcast_in_dim | solution.py:223
  197.3 6.0 %all-to-all-start.1 = ((f32[1,768,1152]{2,0,1:T(1,128)}), f32[1,768,1152]{2,0,1:T(1,128)S(1)}, u32[]{:S(2)}, u32[]{:S(2)}) async-start(f32[1,768,1152]{2,0,1:T(1,128)} %copy.119), calls=%async_computation.4 | async-start | bytes 7077888 | tf_op jit(solution)/shard_map/all_to_all | solution.py:223
  203.3 2.2 multiply_convert_fusion.1
  206.4 3.0 convolution_bitcast_fusion
  209.4 12.2 %copy.122 = f32[1,768,1536]{2,0,1:T(1,128)} copy(f32[1,768,1536]{1,2,0:T(8,128)} %convolution_bitcast_fusion) | data formatting | bytes 9437184 | tf_op jit(solution)/shard_map/broadcast_in_dim | solution.py:226
  221.7 58.4 %all-to-all-done.1 = f32[1,768,1152]{2,0,1:T(1,128)S(1)} async-done(((f32[1,768,1152]{2,0,1:T(1,128)}), f32[1,768,1152]{2,0,1:T(1,128)S(1)}, u32[]{:S(2)}, u32[]{:S(2)}) %all-to-all-start.1) | async-done | bytes 3538976 | tf_op jit(solution)/shard_map/all_to_all | solution.py:223
  280.1 6.4 %all-to-all-start.4 = ((f32[1,768,1536]{2,0,1:T(1,128)}), f32[1,768,1536]{2,0,1:T(1,128)}, u32[]{:S(2)}, u32[]{:S(2)}) async-start(f32[1,768,1536]{2,0,1:T(1,128)} %copy.122), calls=%async_computation.7 | async-start | bytes 9437184 | tf_op jit(solution)/shard_map/all_to_all | solution.py:226
  286.6 4.1 convolution_bitcast_fusion.1
  290.7 9.4 %copy.121 = f32[1,768,1536]{2,0,1:T(1,128)} copy(f32[1,768,1536]{2,1,0:T(8,128)} %convolution_bitcast_fusion.1) | data formatting | bytes 9437184 | tf_op jit(solution)/shard_map/broadcast_in_dim | solution.py:224
  300.1 88.5 %all-to-all-done.4 = f32[1,768,1536]{2,0,1:T(1,128)} async-done(((f32[1,768,1536]{2,0,1:T(1,128)}), f32[1,768,1536]{2,0,1:T(1,128)}, u32[]{:S(2)}, u32[]{:S(2)}) %all-to-all-start.4) | async-done | bytes 4718624 | tf_op jit(solution)/shard_map/all_to_all | solution.py:226
  388.6 6.6 %all-to-all-start.3 = ((f32[1,768,1536]{2,0,1:T(1,128)}), f32[1,768,1536]{2,0,1:T(1,128)}, u32[]{:S(2)}, u32[]{:S(2)}) async-start(f32[1,768,1536]{2,0,1:T(1,128)} %copy.121), calls=%async_computation.6 | async-start | bytes 9437184 | tf_op jit(solution)/shard_map/all_to_all | solution.py:224
  395.2 2.8 fusion.51
  399.3 2.4 copy.129
  401.7 2.0 reduce_sum.199
  406.0 11.7 %reduce-scatter.4.cloned.1.call-done = f32[128,768]{1,0:T(8,128)} async-done(((f32[256,768]{1,0:T(8,128)}), f32[128,768]{1,0:T(8,128)}) %reduce-scatter.4.cloned.1.call-update) | async-done | bytes 393232 | tf_op jit(solution)/shard_map/reduce_scatter | solution.py:141
  417.8 2.5 add_add_fusion.2
  420.3 1.4 reduce.27
  421.7 1.4 reshape.269
  423.1 1.6 reduce_sum.197
  424.7 8.5 %psum.7 = f32[4,48]{0,1:T(8,128)} all-reduce(f32[4,48]{0,1:T(8,128)} %bitcast.115), channel_id=1, replica_groups=mesh['dp'=16,'tensor'=2] {'tensor'}, use_global_device_ids=true, to_apply=%region_20.21 | all-reduce | flops 192 | bytes 1536 | tf_op jit(solution)/shard_map/psum | solution.py:234
  433.3 1.6 slice_reduce_fusion
  434.9 2.0 copy.128
  436.9 2.9 reduce_sum.198
  439.8 4.8 copy.131
  444.6 3.3 reduce_sum.204
  447.9 49.3 %all-to-all-done.3 = f32[1,768,1536]{2,0,1:T(1,128)} async-done(((f32[1,768,1536]{2,0,1:T(1,128)}), f32[1,768,1536]{2,0,1:T(1,128)}, u32[]{:S(2)}, u32[]{:S(2)}) %all-to-all-start.3) | async-done | bytes 4718624 | tf_op jit(solution)/shard_map/all_to_all | solution.py:224
  497.2 4.8 copy.130
  502.0 3.3 reduce_sum.200
  (134 shorter events, 23.9 us)
Async XLA Ops:
  7.2 33.2 %copy-start.31 = (s32[1,4]{1,0:T(1,128)S(1)}, s32[1,4]{1,0:T(1,128)}, u32[]{:S(2)}) copy-start(s32[1,4]{1,0:T(1,128)} %param.21) | copy-start | bytes 52
  7.2 33.5 %copy-start.17 = (bf16[128,768]{1,0:T(8,128)(2,1)S(1)}, bf16[128,768]{1,0:T(8,128)(2,1)}, u32[]{:S(2)}) copy-start(bf16[128,768]{1,0:T(8,128)(2,1)} %param.20) | copy-start | bytes 589828
  7.2 40.6 %copy-start.20 = (bf16[384,48]{0,1:T(8,128)(2,1)S(1)}, bf16[384,48]{0,1:T(8,128)(2,1)}, u32[]{:S(2)}) copy-start(bf16[384,48]{0,1:T(8,128)(2,1)} %param.17) | copy-start | bytes 110596
  7.2 70.0 %all-gather.5.cloned.1.call-start = ((), (), s32[]{:S(2)}) async-start(), calls=%async_computation.8 | async-start | bytes 1880064 | tf_op jit(solution)/shard_map/all_gather | solution.py:77
  7.9 87.1 %all-gather.7.cloned.1.call-start = ((), (), s32[]{:S(2)}) async-start(), calls=%async_computation.9 | async-start | bytes 2506752 | tf_op jit(solution)/shard_map/all_gather | solution.py:78
  8.7 129.8 %all-gather.9.cloned.1.call-start = ((), (), s32[]{:S(2)}) async-start(), calls=%async_computation.10 | async-start | bytes 2506752 | tf_op jit(solution)/shard_map/all_gather | solution.py:80
  9.4 148.4 %reduce-scatter.8.cloned.1.call-start = ((), (), s32[]{:S(2)}) async-start(), calls=%async_computation.13 | async-start | bytes 1179648 | tf_op jit(solution)/shard_map/reduce_scatter | solution.py:213
  10.5 22.0 %copy-start.23 = (f32[128]{0:T(128)}, f32[128]{0:T(128)S(1)}, u32[]{:S(2)}) copy-start(f32[128]{0:T(128)S(1)} %broadcast_multiply_fusion) | copy-start | bytes 1540
  11.7 19.7 %copy-start.29 = (f32[128]{0:T(128)}, f32[128]{0:T(128)S(1)}, u32[]{:S(2)}) copy-start(f32[128]{0:T(128)S(1)} %fusion.29) | copy-start | bytes 1540
  11.7 20.9 %copy-start.25 = (f32[128]{0:T(128)}, f32[128]{0:T(128)S(1)}, u32[]{:S(2)}) copy-start(f32[128]{0:T(128)S(1)} %fusion.40) | copy-start | bytes 1540
  40.4 36.9 %copy-start.12 = (bf16[256,768]{1,0:T(8,128)(2,1)}, bf16[256,768]{1,0:T(8,128)(2,1)S(1)}, u32[]{:S(2)}) copy-start(bf16[256,768]{1,0:T(8,128)(2,1)S(1)} %all_gather.29) | copy-start | bytes 1179652
  47.8 101.6 %copy-start.2 = (bf16[256,768]{1,0:T(8,128)(2,1)}, bf16[256,768]{1,0:T(8,128)(2,1)S(1)}, u32[]{:S(2)}) copy-start(bf16[256,768]{1,0:T(8,128)(2,1)S(1)} %all_gather.35) | copy-start | bytes 1179652
  67.7 0.8 copy-start.8
  79.5 1.5 copy-start.10
  80.5 0.6 copy-start.21
  83.1 1.7 copy-start
  83.3 0.8 copy-start.6
  86.5 90.5 %reduce-scatter.6.cloned.1.call-start = ((), (), s32[]{:S(2)}) async-start(), calls=%async_computation.12 | async-start | bytes 1179648 | tf_op jit(solution)/shard_map/reduce_scatter | solution.py:214
  97.6 47.8 %copy-start.4 = (f32[256,1536]{1,0:T(8,128)}, f32[256,1536]{1,0:T(8,128)S(1)}, u32[]{:S(2)}) copy-start(f32[256,1536]{1,0:T(8,128)S(1)} %fusion.50) | copy-start | bytes 4718596
  138.5 7.8 %copy-start.14 = (bf16[768,1536]{1,0:T(8,128)(2,1)S(1)}, bf16[768,1536]{1,0:T(8,128)(2,1)}, u32[]{:S(2)}) copy-start(bf16[768,1536]{1,0:T(8,128)(2,1)} %all-gather.7.cloned.1.call-done) | copy-start | bytes 7077892
  145.4 0.9 copy-start.18
  146.3 1.7 copy-start.22
  149.4 0.7 copy-start.15
  153.1 23.9 %copy-start.1 = (bf16[128,768]{1,0:T(8,128)(2,1)S(1)}, bf16[128,768]{1,0:T(8,128)(2,1)}, u32[]{:S(2)}) copy-start(bf16[128,768]{1,0:T(8,128)(2,1)} %param.11) | copy-start | bytes 589828
  153.1 23.9 %copy-start.24 = (f32[128]{0:T(128)S(1)}, f32[128]{0:T(128)}, u32[]{:S(2)}) copy-start(f32[128]{0:T(128)} %copy-done.23) | copy-start | bytes 1540
  153.1 25.3 %copy-start.30 = (f32[128]{0:T(128)S(1)}, f32[128]{0:T(128)}, u32[]{:S(2)}) copy-start(f32[128]{0:T(128)} %copy-done.29) | copy-start | bytes 1540
  153.1 25.4 %copy-start.26 = (f32[128]{0:T(128)S(1)}, f32[128]{0:T(128)}, u32[]{:S(2)}) copy-start(f32[128]{0:T(128)} %copy-done.25) | copy-start | bytes 1540
  153.1 31.7 %all-to-all-start.2 = ((f32[1,768,384]{2,0,1:T(1,128)}), f32[1,768,384]{2,0,1:T(1,128)S(1)}, u32[]{:S(2)}, u32[]{:S(2)}) async-start(f32[1,768,384]{2,0,1:T(1,128)} %copy.120), calls=%async_computation.5 | async-start | bytes 2359296 | tf_op jit(solution)/shard_map/all_to_all | solution.py:225
  178.4 12.1 %copy-start.7 = (bf16[256,6,3,64]{0,3,2,1:T(8,128)(2,1)S(1)}, bf16[256,6,3,64]{0,3,2,1:T(8,128)(2,1)}, u32[]{:S(2)}) copy-start(bf16[256,6,3,64]{0,3,2,1:T(8,128)(2,1)} %copy-done.6) | copy-start | bytes 1769476
  178.4 12.1 %copy-start.13 = (bf16[256,768]{1,0:T(8,128)(2,1)S(1)}, bf16[256,768]{1,0:T(8,128)(2,1)}, u32[]{:S(2)}) copy-start(bf16[256,768]{1,0:T(8,128)(2,1)} %copy-done.12) | copy-start | bytes 1179652
  178.4 2.2 copy-start.27
  178.4 2.2 copy-start.28
  184.8 6.4 %copy-start.11 = (f32[1,768,384]{2,0,1:T(1,128)}, f32[1,768,384]{2,0,1:T(1,128)S(1)}, u32[]{:S(2)}) copy-start(f32[1,768,384]{2,0,1:T(1,128)S(1)} %all-to-all-done.2) | copy-start | bytes 3538948
  184.8 11.9 %all-to-all-start = ((f32[16,1,192]{2,1,0:T(1,128)}), f32[16,1,192]{2,1,0:T(1,128)S(1)}, u32[]{:S(2)}, u32[]{:S(2)}) async-start(f32[16,1,192]{2,1,0:T(1,128)} %reshape.268), calls=%async_computation.3 | async-start | bytes 32768 | tf_op jit(solution)/shard_map/all_to_all | solution.py:227
  196.7 0.6 copy-start.19
  197.3 82.8 %all-to-all-start.1 = ((f32[1,768,1152]{2,0,1:T(1,128)}), f32[1,768,1152]{2,0,1:T(1,128)S(1)}, u32[]{:S(2)}, u32[]{:S(2)}) async-start(f32[1,768,1152]{2,0,1:T(1,128)} %copy.119), calls=%async_computation.4 | async-start | bytes 7077888 | tf_op jit(solution)/shard_map/all_to_all | solution.py:223
  203.3 3.1 copy-start.3
  205.5 0.9 copy-start.5
  280.1 108.5 %all-to-all-start.4 = ((f32[1,768,1536]{2,0,1:T(1,128)}), f32[1,768,1536]{2,0,1:T(1,128)}, u32[]{:S(2)}, u32[]{:S(2)}) async-start(f32[1,768,1536]{2,0,1:T(1,128)} %copy.122), calls=%async_computation.7 | async-start | bytes 9437184 | tf_op jit(solution)/shard_map/all_to_all | solution.py:226
  388.6 108.6 %all-to-all-start.3 = ((f32[1,768,1536]{2,0,1:T(1,128)}), f32[1,768,1536]{2,0,1:T(1,128)}, u32[]{:S(2)}, u32[]{:S(2)}) async-start(f32[1,768,1536]{2,0,1:T(1,128)} %copy.121), calls=%async_computation.6 | async-start | bytes 9437184 | tf_op jit(solution)/shard_map/all_to_all | solution.py:224
  395.2 22.6 %reduce-scatter.4.cloned.1.call-start = ((), (), s32[]{:S(2)}) async-start(), calls=%async_computation.11 | async-start | bytes 1179648 | tf_op jit(solution)/shard_map/reduce_scatter | solution.py:141
  395.2 2.8 copy-start.9
  395.2 2.8 copy-start.16
Sparse Core Ops, SparseCore 0:
  10.2 40.4 all-gather.4
  53.0 42.0 all-gather.6
  97.3 41.0 all-gather.8
  140.6 16.7 reduce-scatter.7
  159.6 17.4 reduce-scatter.5
  399.5 18.2 reduce-scatter.3
where the time goes:
time: 516 us; the launch traced here: 512 us
  waiting for transfers between devices  279 us (54%)
  blocking collectives  70 us (14%)
  local copies, waits for them, and re-layouts  55.2 us (11%)
  other arithmetic  32.1 us (6%)
  matrix products  31 us (6%)
  starting transfers between devices  29.7 us (6%)
  between operations  14.7 us (3%)
    all_to_all x1, waiting for transfers between devices, per_device(): lax.all_to_all(grad_down_t[None], 'dp', split_axis=1, concat_axis=0, tile...  88.5 us
    all_to_all x1, waiting for transfers between devices, per_device(): lax.all_to_all(grad_qkv[None], 'dp', split_axis=1, concat_axis=0, tiled=T...  58.4 us
    all_to_all x1, waiting for transfers between devices, per_device(): lax.all_to_all(grad_up[None], 'dp', split_axis=1, concat_axis=0, tiled=True)  49.3 us
    all_gather x1, waiting for transfers between devices, per_device(): lax.all_gather(w_down, 'dp', axis=1, tiled=True)  40.8 us
    unnamed x71, local copies, waits for them, and re-layouts  22.9 us
    all_gather x1, blocking collectives, per_device(): lax.all_gather(w_out, 'dp', axis=1, tiled=True)  19.8 us
    reduce_scatter x1, waiting for transfers between devices, per_device(): lax.psum_scatter(norm_two_grad, 'tensor', scatter_dimension=0, tiled=True)  19.2 us
    dot_general x8, matrix products, contract(): lax.dot_general(first_op, second_op, (((first_dim,), (second_dim,)), ((),...  18.8 us
  transfers between devices with their start and end apart: 11, of which 8 were waited for; matrix products, arithmetic and copies ran while one was open for 20% of the time, Pallas kernels for 0%

commit v1 on v0

--- a/solution.py
+++ b/solution.py
@@ -3,6 +3,8 @@
 import jax
 import jax.numpy as jnp
 from jax import lax
+from jax.experimental import pallas as pl
+from jax.experimental.pallas import tpu as pltpu
 from jax.sharding import PartitionSpec as P
 
 HEAD = 64
@@ -246,6 +248,590 @@
     )
 
 
+MESH = pl.DeviceIdType.MESH
+FIRST = (0, 32)
+SECOND = (32, 16)
+
+
+def place_of():
+    me = lax.axis_index("dp")
+    return me // 4, lax.rem(me // 2, 2), lax.rem(me, 2), lax.axis_index("tensor")
+
+
+def flat(z, x, core):
+    return z * 4 + x * 2 + core
+
+
+def greet(z, x, core, side):
+    barrier = pltpu.get_barrier_semaphore()
+
+    def hello(dp, tensor):
+        pl.semaphore_signal(barrier, inc=1, device_id=(dp, tensor), device_id_type=MESH)
+
+    hello(flat(z, 1 - x, core), side)
+    hello(flat(z, x, 1 - core), side)
+    hello(flat(z, x, core), 1 - side)
+
+    @pl.when(z > 0)
+    def _():
+        hello(flat(z - 1, x, core), side)
+
+    @pl.when(z < 3)
+    def _():
+        hello(flat(z + 1, x, core), side)
+
+    edge = jnp.where((z == 0) | (z == 3), 1, 0)
+    pl.semaphore_wait(barrier, 5 - edge)
+
+
+class Sender:
+    def __init__(self, send_sem):
+        self.send_sem = send_sem
+        self.count = 0
+        self.pending = []
+
+    def send(self, source, target, arrive, dp, tensor, cond, like):
+        copy = pltpu.make_async_remote_copy(
+            src_ref=source,
+            dst_ref=target,
+            send_sem=self.send_sem.at[self.count],
+            recv_sem=arrive,
+            device_id=(dp, tensor),
+            device_id_type=MESH,
+        )
+        self.pending.append((self.count, cond, like))
+        self.count += 1
+        copy.start()
+
+    def drain(self):
+        me, side = lax.axis_index("dp"), lax.axis_index("tensor")
+        for index, cond, like in self.pending:
+
+            def finish():
+                pltpu.make_async_remote_copy(
+                    src_ref=like(),
+                    dst_ref=like(),
+                    send_sem=self.send_sem.at[index],
+                    recv_sem=self.send_sem.at[index],
+                    device_id=(me, side),
+                    device_id_type=MESH,
+                ).wait_send()
+
+            if cond is None:
+                finish()
+            else:
+                pl.when(cond())(finish)
+
+
+def gather_kernel(shard, tok, cot, full, tok_all, cot_all, send_sem, recv_sem, local_sem):
+    z, x, core, side = place_of()
+    me = flat(z, x, core)
+    greet(z, x, core, side)
+    sender = Sender(send_sem)
+    ids = {}
+
+    def arrive(*name):
+        return recv_sem.at[ids.setdefault(name, len(ids))]
+
+    def part(ref, index, rows):
+        return ref.at[index, pl.ds(rows[0], rows[1]), :]
+
+    def shard_part(index, rows, own):
+        return shard.at[pl.ds(rows[0], rows[1]), :] if own else part(full, index, rows)
+
+    def move(index, rows, name, dp, tensor, cond, own):
+        sender.send(
+            shard_part(index, rows, own),
+            part(full, index, rows),
+            arrive(*name),
+            dp,
+            tensor,
+            cond,
+            lambda: part(full, 0, rows),
+        )
+
+    def await_part(index, rows, name):
+        here = part(full, index, rows)
+        pltpu.make_async_remote_copy(
+            src_ref=here,
+            dst_ref=here,
+            send_sem=send_sem.at[0],
+            recv_sem=arrive(*name),
+            device_id=(me, side),
+            device_id_type=MESH,
+        ).wait_recv()
+
+    def along(way, near, rows, index, other, cond, own):
+        def both():
+            inside = z < 3 if way > 0 else z > 0
+            return inside if cond is None else inside & cond()
+
+        @pl.when(z < 3 if way > 0 else z > 0)
+        def _():
+            move(index, rows, ("z", way, near, rows, other), flat(z + way, x, core), side, both, own)
+
+    def across(index, rows, distance, cond, own):
+        move(index, rows, ("x", rows, distance), flat(z, 1 - x, core), side, cond, own)
+
+    def sibling(index, rows, name, cond, own):
+        move(index, rows, ("c", rows) + name, flat(z, x, 1 - core), side, cond, own)
+
+    half = tok.shape[0]
+    mine = pl.ds(side * half, half)
+    own_copies = [
+        pltpu.make_async_copy(shard, full.at[me], local_sem.at[0]),
+        pltpu.make_async_copy(tok, tok_all.at[mine, :], local_sem.at[1]),
+        pltpu.make_async_copy(cot, cot_all.at[mine, :], local_sem.at[2]),
+    ]
+    for way in (1, -1):
+        along(way, 1, FIRST, me, 0, None, True)
+    across(me, SECOND, 0, None, True)
+    across(me, FIRST, 0, None, True)
+    for way in (1, -1):
+        along(way, 1, SECOND, me, 0, None, True)
+    sender.send(tok, tok_all.at[mine, :], arrive("tok"), me, 1 - side, None, lambda: tok)
+    sender.send(cot, cot_all.at[mine, :], arrive("cot"), me, 1 - side, None, lambda: cot)
+    sibling(me, FIRST, (0, 0), None, True)
+    sibling(me, SECOND, (0, 0), None, True)
+    for copy in own_copies:
+        copy.start()
+
+    other_here = flat(z, 1 - x, core)
+    await_part(other_here, SECOND, ("x", SECOND, 0))
+    for way in (1, -1):
+        along(way, 1, SECOND, other_here, 1, None, False)
+    sibling(other_here, SECOND, (0, 1), None, False)
+
+    def from_x(distance):
+        index = flat(z + distance, 1 - x, core)
+        if distance == 0:
+            await_part(index, FIRST, ("x", FIRST, distance))
+            sibling(index, FIRST, (distance, 1), None, False)
+        else:
+            def cond():
+                return (z + distance >= 0) & (z + distance <= 3)
+
+            @pl.when(cond())
+            def _():
+                await_part(index, FIRST, ("x", FIRST, distance))
+                sibling(index, FIRST, (distance, 1), cond, False)
+
+    for near in (1, 2, 3):
+        for rows, other in ((FIRST, 0), (SECOND, 0), (SECOND, 1)):
+            for way in (1, -1):
+                def cond(way=way, near=near):
+                    return (z - near >= 0) if way > 0 else (z + near <= 3)
+
+                @pl.when(cond())
+                def _():
+                    index = flat(z - way * near, x if other == 0 else 1 - x, core)
+                    await_part(index, rows, ("z", way, near, rows, other))
+                    if near < 3:
+                        along(way, near + 1, rows, index, other, cond, False)
+                    if rows == FIRST:
+                        across(index, rows, -way * near, cond, False)
+                    sibling(index, rows, (-way * near, other), cond, False)
+
+        if near == 1:
+            from_x(0)
+        else:
+            from_x(near - 1)
+            from_x(1 - near)
+    from_x(3)
+    from_x(-3)
+
+    for distance in range(-3, 4):
+        for other in (0, 1):
+            for rows in (FIRST, SECOND):
+
+                def take():
+                    index = flat(z + distance, x if other == 0 else 1 - x, 1 - core)
+                    await_part(index, rows, ("c", rows, distance, other))
+
+                if distance == 0:
+                    take()
+                else:
+                    pl.when((z + distance >= 0) & (z + distance <= 3))(take)
+    theirs = pl.ds((1 - side) * half, half)
+    for name, ref in (("tok", tok_all), ("cot", cot_all)):
+        here = ref.at[theirs, :]
+        pltpu.make_async_remote_copy(
+            src_ref=here,
+            dst_ref=here,
+            send_sem=send_sem.at[0],
+            recv_sem=arrive(name),
+            device_id=(me, side),
+            device_id_type=MESH,
+        ).wait_recv()
+    for copy in own_copies:
+        copy.wait()
+    sender.drain()
+
+
+def gather_all(shard, tok, cot):
+    rows, width = shard.shape
+    vmem = pl.BlockSpec(memory_space=pltpu.VMEM)
+    return pl.pallas_call(
+        gather_kernel,
+        out_shape=(
+            jax.ShapeDtypeStruct((16, rows, width), shard.dtype),
+            jax.ShapeDtypeStruct((2 * tok.shape[0], tok.shape[1]), tok.dtype),
+            jax.ShapeDtypeStruct((2 * cot.shape[0], cot.shape[1]), cot.dtype),
+        ),
+        in_specs=[vmem] * 3,
+        out_specs=(vmem,) * 3,
+        scratch_shapes=[
+            pltpu.SemaphoreType.DMA((80,)),
+            pltpu.SemaphoreType.DMA((80,)),
+            pltpu.SemaphoreType.DMA((3,)),
+        ],
+        compiler_params=pltpu.CompilerParams(
+            collective_id=0, has_side_effects=True, vmem_limit_bytes=40 * 1024 * 1024
+        ),
+        name="gather_all",
+    )(shard, tok, cot)
+
+
+def reduce_kernel(
+    parts, to_peer, total, from_peer, sums, from_core, from_x, up, down, last_x, norm_send,
+    norm_recv, send_sem, recv_sem
+):
+    z, x, core, side = place_of()
+    me = flat(z, x, core)
+    greet(z, x, core, side)
+    sender = Sender(send_sem)
+    ids = {}
+    width = parts.shape[2]
+    a_rows, b_rows = pl.ds(*FIRST), pl.ds(*SECOND)
+
+    def arrive(*name):
+        return recv_sem.at[ids.setdefault(name, len(ids))]
+
+    def await_at(ref, *name):
+        pltpu.make_async_remote_copy(
+            src_ref=ref,
+            dst_ref=ref,
+            send_sem=send_sem.at[0],
+            recv_sem=arrive(*name),
+            device_id=(me, side),
+            device_id_type=MESH,
+        ).wait_recv()
+
+    def add(target, left, right, rows):
+        @pl.loop(0, rows // 16)
+        def _(step):
+            at = pl.ds(pl.multiple_of(step * 16, 16), 16)
+            target[at, :] = left[at, :] + right[at, :]
+
+    def zq(q):
+        return jnp.where(z < 2, q, 3 - q)
+
+    order = [(q, other) for q in (3, 2, 1, 0) for other in (1, 0)]
+
+    def x_of(other):
+        return 1 - x if other else x
+
+    for q, other in order:
+        sender.send(
+            parts.at[flat(zq(q), x_of(other), 1 - core)],
+            from_core.at[q * 2 + other],
+            arrive("c", q, other),
+            flat(z, x, 1 - core),
+            side,
+            None,
+            lambda: parts.at[0],
+        )
+    sender.send(to_peer, from_peer, arrive("y"), me, 1 - side, None, lambda: to_peer)
+
+    def slot(q, other):
+        return q * 2 + other
+
+    def q_of(far):
+        return jnp.where(z < 2, z + far, 3 - z - far)
+
+    def buffers(way):
+        return up if way > 0 else down
+
+    def chain_send(way, far, kind, block, cond):
+        other = 1 if kind == 2 else 0
+        rows = a_rows if kind == 0 else b_rows
+        buffer = buffers(way)
+        base, count = ((0, 32), (32, 16), (48, 16))[kind]
+        sender.send(
+            sums.at[block, rows, :],
+            buffer.at[far - 1, pl.ds(base, count), :],
+            arrive("z", way, far - 1, kind),
+            flat(z + way, x, core),
+            side,
+            cond,
+            lambda: sums.at[0, rows, :],
+        )
+
+    def chain_add(way, far, kind, block):
+        rows = a_rows if kind == 0 else b_rows
+        base, count = ((0, 32), (32, 16), (48, 16))[kind]
+        got = buffers(way).at[far, pl.ds(base, count), :]
+        await_at(got, "z", way, far, kind)
+        here = sums.at[block, rows, :]
+        add(here, here, got, count)
+
+    def take_x(q):
+        await_at(from_x.at[q], "x", q)
+        here = sums.at[slot(q, 0), a_rows, :]
+        add(here, here, from_x.at[q], FIRST[1])
+
+    for q, other in order:
+        await_at(from_core.at[q * 2 + other], "c", q, other)
+        add(
+            sums.at[slot(q, other)],
+            parts.at[flat(zq(q), x_of(other), core)],
+            from_core.at[q * 2 + other],
+            48,
+        )
+        if other:
+            sender.send(
+                sums.at[slot(q, 1), a_rows, :],
+                from_x.at[q],
+                arrive("x", q),
+                flat(z, 1 - x, core),
+                side,
+                None,
+                lambda: sums.at[0, a_rows, :],
+            )
+        else:
+            for way in (1, -1):
+                if q > 0:
+                    def cond(way=way):
+                        return (z == 0) if way > 0 else (z == 3)
+
+                    @pl.when(cond())
+                    def _():
+                        chain_send(way, q, 1, slot(q, 0), cond)
+                        chain_send(way, q, 2, slot(q, 1), cond)
+
+            if q < 3:
+                take_x(q + 1)
+                for way in (1, -1):
+                    def cond(way=way):
+                        return (z == 0) if way > 0 else (z == 3)
+
+                    @pl.when(cond())
+                    def _():
+                        chain_send(way, q + 1, 0, slot(q + 1, 0), cond)
+
+    take_x(0)
+    for far in (2, 1):
+        for kind in (1, 2, 0):
+            for way in (1, -1):
+                def middle(way=way, far=far):
+                    return ((z > 0) & (z + far <= 3)) if way > 0 else ((z < 3) & (z - far >= 0))
+
+                @pl.when(middle())
+                def _():
+                    q = q_of(way * far)
+                    block = q * 2 + (1 if kind == 2 else 0)
+                    chain_add(way, far, kind, block)
+                    chain_send(way, far, kind, block, middle)
+
+    own_q = jnp.where(z < 2, z, 3 - z)
+    for kind in (2, 1, 0):
+        block = own_q * 2 + (1 if kind == 2 else 0)
+        for way in (1, -1):
+            has = (z > 0) if way > 0 else (z < 3)
+
+            @pl.when(has)
+            def _():
+                chain_add(way, 0, kind, block)
+
+        if kind == 2:
+            sender.send(
+                sums.at[block, b_rows, :],
+                last_x,
+                arrive("lx"),
+                flat(z, 1 - x, core),
+                side,
+                None,
+                lambda: last_x,
+            )
+    own = own_q * 2
+    norm_at = width - 128
+
+    @pl.loop(0, 2)
+    def _(step):
+        at = pl.ds(pl.multiple_of(step * 16, 16), 16)
+        total[at, :] = sums[own, at, :].astype(jnp.float32)
+
+    await_at(last_x, "lx")
+    total[32:48, :] = sums[own, 32:48, :].astype(jnp.float32) + last_x[...].astype(jnp.float32)
+    norm_send[...] = total[:, norm_at:]
+    sender.send(norm_send, norm_recv, arrive("n"), me, 1 - side, None, lambda: norm_send)
+    await_at(norm_recv, "n")
+    total[:, norm_at:] = norm_send[...] + norm_recv[...]
+    await_at(from_peer, "y")
+    sender.drain()
+
+
+def reduce_all(parts, to_peer):
+    _, rows, width = parts.shape
+    vmem = pl.BlockSpec(memory_space=pltpu.VMEM)
+    low = parts.dtype
+    return pl.pallas_call(
+        reduce_kernel,
+        out_shape=(
+            jax.ShapeDtypeStruct((rows, width), jnp.float32),
+            jax.ShapeDtypeStruct(to_peer.shape, to_peer.dtype),
+        ),
+        in_specs=[vmem] * 2,
+        out_specs=(vmem,) * 2,
+        scratch_shapes=[
+            pltpu.VMEM((8, rows, width), low),
+            pltpu.VMEM((8, rows, width), low),
+            pltpu.VMEM((4, FIRST[1], width), low),
+            pltpu.VMEM((3, 64, width), low),
+            pltpu.VMEM((3, 64, width), low),
+            pltpu.VMEM((SECOND[1], width), low),
+            pltpu.VMEM((rows, 128), jnp.float32),
+            pltpu.VMEM((rows, 128), jnp.float32),
+            pltpu.SemaphoreType.DMA((64,)),
+            pltpu.SemaphoreType.DMA((64,)),
+        ],
+        compiler_params=pltpu.CompilerParams(
+            collective_id=1, has_side_effects=True, vmem_limit_bytes=48 * 1024 * 1024
+        ),
+        name="reduce_all",
+    )(parts, to_peer)
+
+
+def plain_norm(values):
+    center = values - jnp.mean(values, axis=-1, keepdims=True)
+    spread = jnp.mean(center * center, axis=-1, keepdims=True)
+    inverse = lax.rsqrt(spread + norm_eps)
+    return center * inverse, inverse
+
+
+def middle(tok_all, cot_all, weights, norm_float, lengths_row):
+    rows = tok_all.shape[0]
+    qkv_w, up_w, out_t, down_t = weights
+    heads = qkv_w.shape[1] // (3 * HEAD)
+    scale = 1.0 / math.sqrt(HEAD)
+    gain_one, bias_one, gain_two, bias_two = (norm_float[i][None, :] for i in range(4))
+    segment, positions, places = doc_layout(lengths_row, rows)
+    wave_cos, wave_sin = rope_tables(positions)
+    xhat, _ = plain_norm(tok_all.astype(jnp.float32))
+    normed_one = (xhat * gain_one + bias_one).astype(jnp.bfloat16)
+    normed_two = (xhat * gain_two + bias_two).astype(jnp.bfloat16)
+    projected = contract(normed_one, qkv_w, 1, 0).reshape(rows, heads, 3, HEAD)
+    queries = rotate(projected[:, :, 0], wave_cos, wave_sin).astype(jnp.bfloat16)
+    keys = rotate(projected[:, :, 1], wave_cos, wave_sin).astype(jnp.bfloat16)
+    values = projected[:, :, 2].astype(jnp.bfloat16)
+    allowed = (segment[:, None] == segment[None, :]) & (places[:, None] >= places[None, :])
+    f32 = jnp.float32
+    scores = jnp.einsum("qhd,khd->hqk", queries, keys, preferred_element_type=f32) * scale
+    scores = jnp.where(allowed[None], scores, masked_score)
+    exponent = jnp.exp(scores - jnp.max(scores, axis=-1, keepdims=True))
+    prob = exponent / jnp.sum(exponent, axis=-1, keepdims=True)
+    prob_low = prob.astype(jnp.bfloat16)
+    attended = jnp.einsum("hqk,khd->qhd", prob_low, values, preferred_element_type=f32)
+    attended = attended.astype(jnp.bfloat16).reshape(rows, heads * HEAD)
+    hidden = contract(normed_two, up_w, 1, 0)
+    cdf = 0.5 * (1.0 + lax.erf(hidden * math.sqrt(0.5)))
+    activated = (hidden * cdf).astype(jnp.bfloat16)
+    branch = contract(attended, out_t, 1, 1) + contract(activated, down_t, 1, 1)
+    slope = cdf + hidden * jnp.exp(-0.5 * hidden * hidden) * (1.0 / math.sqrt(2.0 * math.pi))
+    pre_grad = (slope * contract(cot_all, down_t, 1, 0)).astype(jnp.bfloat16)
+    att_grad = contract(cot_all, out_t, 1, 0).astype(jnp.bfloat16).reshape(rows, heads, HEAD)
+    prob_grad = jnp.einsum("qhd,khd->hqk", att_grad, values, preferred_element_type=f32)
+    row_dot = jnp.sum(prob * prob_grad, axis=-1, keepdims=True)
+    score_grad = (prob * (prob_grad - row_dot)).astype(jnp.bfloat16)
+    query_grad = jnp.einsum("hqk,khd->qhd", score_grad, keys, preferred_element_type=f32) * scale
+    key_grad = jnp.einsum("hqk,qhd->khd", score_grad, queries, preferred_element_type=f32) * scale
+    value_grad = jnp.einsum("hqk,qhd->khd", prob_low, att_grad, preferred_element_type=f32)
+    proj_grad = jnp.stack(
+        [
+            rotate(query_grad, wave_cos, -wave_sin),
+            rotate(key_grad, wave_cos, -wave_sin),
+            value_grad,
+        ],
+        axis=2,
+    )
+    proj_grad = proj_grad.reshape(rows, 3 * heads * HEAD).astype(jnp.bfloat16)
+    norm_one_grad = contract(proj_grad, qkv_w, 1, 1)
+    norm_two_grad = contract(pre_grad, up_w, 1, 1)
+    norm_sums = jnp.stack(
+        [
+            jnp.sum(norm_one_grad * xhat, axis=0),
+            jnp.sum(norm_one_grad, axis=0),
+            jnp.sum(norm_two_grad * xhat, axis=0),
+            jnp.sum(norm_two_grad, axis=0),
+        ],
+        axis=1,
+    )
+    low = jnp.bfloat16
+    grads = jnp.concatenate(
+        [
+            contract(normed_one, proj_grad, 0, 0).astype(low),
+            contract(normed_two, pre_grad, 0, 0).astype(low),
+            contract(cot_all, attended, 0, 0).astype(low),
+            contract(cot_all, activated, 0, 0).astype(low),
+            jnp.pad(norm_sums, ((0, 0), (0, 124))).astype(low),
+        ],
+        axis=1,
+    )
+    return grads, branch, norm_one_grad, norm_two_grad
+
+
+def line_device(
+    tokens, ln1_gain, ln1_bias, ln2_gain, ln2_bias, w_qkv, w_out, w_up, w_down, grad_out, lengths
+):
+    half = tokens.shape[0]
+    side = lax.axis_index("tensor")
+    norm_params = jnp.stack([ln1_gain, ln1_bias, ln2_gain, ln2_bias], axis=1)
+    shard = jnp.concatenate(
+        [w_qkv, w_up, w_out.T, w_down.T, jnp.pad(norm_params, ((0, 0), (0, 124)))], axis=1
+    )
+    cuts = []
+    for piece in (w_qkv.shape[1], w_up.shape[1], w_out.shape[0], w_down.shape[0]):
+        cuts.append((cuts[-1] if cuts else 0) + piece)
+    full, tok_all, cot_all = gather_all(shard, tokens, grad_out)
+    full = full.reshape(-1, full.shape[2])
+    weights = (
+        full[:, : cuts[0]],
+        full[:, cuts[0] : cuts[1]],
+        full[:, cuts[1] : cuts[2]],
+        full[:, cuts[2] : cuts[3]],
+    )
+    norm_float = full[:, cuts[3] : cuts[3] + 4].astype(jnp.float32).T
+    grads, branch, one_grad, two_grad = middle(tok_all, cot_all, weights, norm_float, lengths[0])
+    stacked = jnp.stack([branch, one_grad, two_grad], axis=0).reshape(3, 2, half, -1)
+    to_peer = lax.dynamic_index_in_dim(stacked, 1 - side, 1, False).astype(jnp.bfloat16)
+    own = lax.dynamic_index_in_dim(stacked, side, 1, False)
+    total, from_peer = reduce_all(grads.reshape(16, -1, grads.shape[1]), to_peer)
+    summed = own + from_peer.astype(jnp.float32)
+    tokens_f = tokens.astype(jnp.float32)
+    output = (tokens_f + summed[0]).astype(jnp.bfloat16)
+    xhat, inverse = plain_norm(tokens_f)
+    grad = summed[1] * norm_float[0][None, :] + summed[2] * norm_float[2][None, :]
+    row_grad = inverse * (
+        grad
+        - jnp.mean(grad, axis=-1, keepdims=True)
+        - xhat * jnp.mean(grad * xhat, axis=-1, keepdims=True)
+    )
+    grad_tokens = grad_out.astype(jnp.float32) + row_grad
+    norm_total = total[:, cuts[3] : cuts[3] + 4].T
+    return (
+        output,
+        grad_tokens,
+        norm_total[0],
+        norm_total[1],
+        norm_total[2],
+        norm_total[3],
+        total[:, : cuts[0]],
+        total[:, cuts[1] : cuts[2]].T,
+        total[:, cuts[0] : cuts[1]],
+        total[:, cuts[2] : cuts[3]].T,
+    )
+
+
 def solution(mesh):
     placed = (
         P(("dp", "tensor"), None),
@@ -260,8 +846,9 @@
         P(("dp", "tensor"), None),
         P("dp", None),
     )
+    body = line_device if mesh.shape["dp"] == 16 and mesh.shape["tensor"] == 2 else per_device
     return jax.shard_map(
-        per_device,
+        body,
         mesh=mesh,
         in_specs=placed,
         out_specs=(

time: 516 us -> 166 us (0.32)
  waiting for transfers between devices: 279 us -> 0 us
  Pallas kernels: 0 us -> 113 us
  blocking collectives: 70 us -> 0 us
  local copies, waits for them, and re-layouts: 55.2 us -> 22.1 us
  starting transfers between devices: 29.7 us -> 0 us
  other arithmetic: 32.1 us -> 7.35 us
  between operations: 14.7 us -> 1.4 us
  matrix products: 31 us -> 22.3 us
    all_to_all x5 -> x0, waiting for transfers between devices: 197 us -> none  [the longest x1 88.5 us: per_device(): lax.all_to_all(grad_down_t[None], 'dp', split_axis=1, concat_axis=0, tile...]
    pallas_call x0 -> x2, Pallas kernels: none -> 113 us  [the longest x1 70.5 us: reduce_all(): pl.pallas_call(reduce_kernel, out_shape=(jax.ShapeDtypeStruct((rows, widt...]
    all_gather x5 -> x0, blocking collectives: 61.5 us -> none  [the longest x1 19.8 us: per_device(): lax.all_gather(w_out, 'dp', axis=1, tiled=True)]
    all_gather x3 -> x0, waiting for transfers between devices: 49.4 us -> none  [the longest x1 40.8 us: per_device(): lax.all_gather(w_down, 'dp', axis=1, tiled=True)]
    reduce_scatter x3 -> x0, waiting for transfers between devices: 30.9 us -> none  [the longest x1 19.2 us: per_device(): lax.psum_scatter(norm_two_grad, 'tensor', scatter_dimension=0, tiled=True)]
    broadcast_in_dim x5 -> x0, local copies, waits for them, and re-layouts: 30.1 us -> none  [the longest x1 12.2 us: per_device(): grad_down_t[None]]
    all_to_all x5 -> x0, starting transfers between devices: 29.4 us -> none  [the longest x1 6.55 us: per_device(): lax.all_to_all(grad_up[None], 'dp', split_axis=1, concat_axis=0, tiled=True)]
    reduce_sum x10 -> x5, other arithmetic: 19 us -> 1.53 us  [the longest x1 0.85 us: line_device(): jnp.mean(grad, axis=-1, keepdims=True)]
  transfers between devices with their start and end apart: 11 -> 0, of which waited for: 8 -> 0; matrix products, arithmetic and copies ran while one was open for 20% -> 0% of each run, Pallas kernels for 0% -> 0%
where the time goes in v1:
time: 166 us
  Pallas kernels  113 us (68%)
  matrix products  22.3 us (13%)
  local copies, waits for them, and re-layouts  22.1 us (13%)
  other arithmetic  7.35 us (4%)
    pallas_call x1, Pallas kernels, reduce_all(): pl.pallas_call(reduce_kernel, out_shape=(jax.ShapeDtypeStruct((rows, widt...  70.5 us
    pallas_call x1, Pallas kernels, gather_all(): pl.pallas_call(gather_kernel, out_shape=(jax.ShapeDtypeStruct((16, rows,...  42 us
    dot_general x12, matrix products, contract(): lax.dot_general(first_op, second_op, (((first_dim,), (second_dim,)), ((),...  17.8 us
    unnamed x77, local copies, waits for them, and re-layouts  14.8 us

profile of v1, /device:TPU:8, one launch (start us, length us, event | category | flops | bytes accessed | tf_op | source)
XLA Modules:
  0.0 165.7 jit_solution(9204785246936120334)
XLA Ops:
  0.6 0.9 constant_dynamic-update-slice_fusion.2
  1.6 0.9 constant_dynamic-update-slice_fusion.1
  2.5 0.8 bitcast_dynamic-update-slice_fusion.1
  3.3 0.9 bitcast_dynamic-update-slice_fusion
  4.2 0.7 pad_maximum_fusion.5
  5.0 0.9 copy-done
  6.0 0.9 copy-done.2
  6.9 42.0 %gather_all.1 = (bf16[16,48,4736]{2,1,0:T(8,128)(2,1)S(1)}, bf16[256,768]{1,0:T(8,128)(2,1)S(1)}, bf16[256,768]{1,0:T(8,128)(2,1)S(1)}) custom-call(bf16[48,4736]{1,0:T(8,128)(2,1)S(1)} %constant_dynamic-update-slice_fusion.shard, bf16[128,768]{1,0:T(8,128)(2,1)S(1)} %copy-done, bf16[128,768]{1,0:T(8,128)(2,1)S(1)} %copy-done.2), custom_call_target="tpu_custom_call" | custom-call | tf_op jit(solution)/shard_map/gather_all/pallas_call | solution.py:474
  49.0 0.2 fusion.38
  49.3 2.5 %copy-done.4 = bf16[16,48,4736]{2,1,0:T(8,128)(2,1)} copy-done((bf16[16,48,4736]{2,1,0:T(8,128)(2,1)}, bf16[16,48,4736]{2,1,0:T(8,128)(2,1)S(1)}, u32[]{:S(2)}) %copy-start.4) | copy-done | bytes 7274520
  52.0 0.6 slice_reduce_fusion.5
  52.6 2.4 %fusion.19 = f32[256,1152]{0,1:T(8,128)S(1)} fusion(bf16[768,4736]{1,0:T(8,128)(2,1)} %bitcast.93, bf16[256,768]{1,0:T(8,128)(2,1)S(1)} %get-tuple-element.15, f32[768]{0:T(1024)S(1)} %get-tuple-element.34, f32[768]{0:T(1024)S(1)} %get-tuple-element.35, f32[256]{0:T(256)S(1)} %add_rsqrt_fusion, f32[256]{0:T(256)S(1)} %broadcast_multiply_fusion), kind=kOutput, calls=%fused_computation.30 | convolution fusion | flops 454164480 | bytes 3350528 | tf_op jit(solution)/shard_map/dot_general | solution.py:62
  55.2 0.9 copy-done.8
  56.9 0.7 fusion.74
  57.6 1.3 convolution_convert_fusion.6
  59.0 2.5 %fusion.10 = f32[256,1536]{1,0:T(8,128)S(1)} fusion(bf16[768,4736]{1,0:T(8,128)(2,1)} %bitcast.94, bf16[256,768]{1,0:T(8,128)(2,1)S(1)} %get-tuple-element.15, f32[768]{0:T(1024)S(1)} %copy-done.23, f32[768]{0:T(1024)S(1)} %copy-done.14, f32[256]{0:T(256)S(1)} %copy-done.28, f32[256]{0:T(256)S(1)} %copy-done.21), kind=kOutput, calls=%fused_computation.16 | convolution fusion | flops 605159424 | bytes 4333568 | tf_op jit(solution)/shard_map/dot_general | solution.py:62
  61.5 3.1 %fusion.6 = f32[256,768]{1,0:T(8,128)S(1)} fusion(bf16[768,4736]{1,0:T(8,128)(2,1)} %bitcast.95, f32[256,1536]{1,0:T(8,128)S(1)} %fusion.10), kind=kOutput, calls=%fused_computation.12 | convolution fusion | flops 605945856 | bytes 4718592 | tf_op jit(solution)/shard_map/dot_general | solution.py:62
  64.6 1.5 convolution_add_fusion
  66.1 2.1 %convolution_convert_fusion.5 = bf16[256,384]{1,0:T(8,128)(2,1)} fusion(bf16[256,768]{1,0:T(8,128)(2,1)S(1)} %get-tuple-element.17, bf16[768,4736]{1,0:T(8,128)(2,1)} %bitcast.97), kind=kOutput, calls=%fused_computation.43 | convolution fusion | flops 151093248 | bytes 1179648 | tf_op jit(solution)/shard_map/dot_general | solution.py:62
  68.2 1.7 %copy.76 = bf16[256,384]{0,1:T(8,128)(2,1)} copy(bf16[256,384]{1,0:T(8,128)(2,1)} %convolution_convert_fusion.5) | data formatting | bytes 393216 | tf_op jit(solution)/shard_map/convert_element_type | solution.py:742
  70.0 1.5 multiply_reduce_fusion
  71.6 0.3 multiply_convert_fusion
  71.9 0.5 copy-done.7
  72.4 0.3 fusion.24
  72.7 0.4 fusion.23
  73.2 0.4 copy-done.9
  73.6 0.4 fusion.25
  74.1 1.3 slice-done.1
  75.4 0.5 copy-done.32
  76.0 1.4 fusion.4
  77.4 0.8 fusion.8
  78.2 0.9 fusion.36
  79.1 1.6 pad_maximum_fusion
  80.6 1.3 fusion.39.to_peer
  82.3 0.9 fusion.3
  83.2 1.0 fusion.2
  84.1 0.5 fusion.22
  84.6 0.9 fusion.1
  85.6 3.0 %copy-done.5 = bf16[768,4736]{1,0:T(8,128)(2,1)} copy-done((bf16[768,4736]{1,0:T(8,128)(2,1)}, bf16[768,4736]{1,0:T(8,128)(2,1)S(1)}, u32[]{:S(2)}) %copy-start.5) | copy-done | bytes 7274520
  88.6 70.5 %reduce_all.1 = (f32[48,4736]{1,0:T(8,128)S(1)}, bf16[3,128,768]{2,1,0:T(8,128)(2,1)S(1)}) custom-call(bf16[16,48,4736]{2,1,0:T(8,128)(2,1)} %bitcast.103, bf16[3,128,768]{2,1,0:T(8,128)(2,1)S(1)} %fusion.39.to_peer), custom_call_target="tpu_custom_call" | custom-call | tf_op jit(solution)/shard_map/reduce_all/pallas_call | solution.py:678
  159.1 1.4 bitcast_add_fusion
  160.7 0.2 fusion.50
  160.9 0.8 fusion.71
  161.8 0.9 fusion.49
  162.7 0.9 slice_bitcast_fusion.3
  163.6 0.7 slice.147
  164.3 0.6 slice_bitcast_fusion.4
  164.9 0.7 slice_reduce_fusion
  (104 shorter events, 2.0 us)
Async XLA Ops:
  5.0 0.9 copy-start
  6.0 0.9 copy-start.2
  48.9 3.0 %copy-start.4 = (bf16[16,48,4736]{2,1,0:T(8,128)(2,1)}, bf16[16,48,4736]{2,1,0:T(8,128)(2,1)S(1)}, u32[]{:S(2)}) copy-start(bf16[16,48,4736]{2,1,0:T(8,128)(2,1)S(1)} %get-tuple-element.16) | copy-start | bytes 21823492
  49.0 6.0 %copy-start.20 = (f32[256]{0:T(256)}, f32[256]{0:T(256)S(1)}, u32[]{:S(2)}) copy-start(f32[256]{0:T(256)S(1)} %broadcast_multiply_fusion) | copy-start | bytes 3076
  49.3 5.8 %copy-start.27 = (f32[256]{0:T(256)}, f32[256]{0:T(256)S(1)}, u32[]{:S(2)}) copy-start(f32[256]{0:T(256)S(1)} %add_rsqrt_fusion) | copy-start | bytes 3076
  52.6 2.4 %copy-start.16 = (f32[768]{0:T(1024)}, f32[768]{0:T(1024)S(1)}, u32[]{:S(2)}) copy-start(f32[768]{0:T(1024)S(1)} %get-tuple-element.35) | copy-start | bytes 9220
  52.6 2.4 %copy-start.25 = (f32[768]{0:T(1024)}, f32[768]{0:T(1024)S(1)}, u32[]{:S(2)}) copy-start(f32[768]{0:T(1024)S(1)} %get-tuple-element.34) | copy-start | bytes 9220
  55.1 1.0 copy-start.8
  55.1 1.0 copy-start.30
  56.7 0.9 copy-start.10
  56.7 0.9 copy-start.12
  56.7 0.9 copy-start.6
  57.6 1.3 copy-start.18
  57.6 1.3 copy-start.14
  57.6 1.3 copy-start.21
  57.6 1.3 copy-start.23
  57.6 1.3 copy-start.28
  61.5 3.1 %copy-start.31 = (f32[256,1536]{1,0:T(8,128)}, f32[256,1536]{1,0:T(8,128)S(1)}, u32[]{:S(2)}) copy-start(f32[256,1536]{1,0:T(8,128)S(1)} %fusion.10) | copy-start | bytes 4718596
  70.0 1.6 copy-start.19
  71.5 0.9 copy-start.7
  71.5 0.9 copy-start.11
  71.5 0.9 copy-start.13
  71.5 2.6 %slice-start = ((s8[7274496]{0:T(1024)(128)(4,1)}), s8[3080192]{0:T(1024)(128)(4,1)S(1)}, s32[]{:S(2)}) async-start(s8[7274496]{0:T(1024)(128)(4,1)} %bitcast.98), calls=%async_computation | async-start | bytes 6160384
  72.7 0.9 copy-start.9
  73.2 2.3 %slice-start.1 = ((s8[7274496]{0:T(1024)(128)(4,1)}), s8[4194304]{0:T(1024)(128)(4,1)S(1)}, s32[]{:S(2)}) async-start(s8[7274496]{0:T(1024)(128)(4,1)} %bitcast.98), calls=%async_computation.1 | async-start | bytes 8388608
  74.0 2.0 %copy-start.32 = (f32[256,1536]{1,0:T(8,128)S(1)}, f32[256,1536]{1,0:T(8,128)}, u32[]{:S(2)}) copy-start(f32[256,1536]{1,0:T(8,128)} %copy-done.31) | copy-start | bytes 4718596
  77.3 0.8 copy-start.22
  77.3 0.8 copy-start.29
  79.0 3.2 %copy-start.17 = (f32[768]{0:T(1024)S(1)}, f32[768]{0:T(1024)}, u32[]{:S(2)}) copy-start(f32[768]{0:T(1024)} %copy-done.16) | copy-start | bytes 9220
  79.1 3.2 %copy-start.26 = (f32[768]{0:T(1024)S(1)}, f32[768]{0:T(1024)}, u32[]{:S(2)}) copy-start(f32[768]{0:T(1024)} %copy-done.25) | copy-start | bytes 9220
  82.3 0.9 copy-start.15
  82.3 0.9 copy-start.24
  83.2 1.5 copy-start.33
  85.6 3.0 %copy-start.5 = (bf16[768,4736]{1,0:T(8,128)(2,1)}, bf16[768,4736]{1,0:T(8,128)(2,1)S(1)}, u32[]{:S(2)}) copy-start(bf16[768,4736]{1,0:T(8,128)(2,1)S(1)} %pad_dynamic-update-slice_fusion) | copy-start | bytes 21823492
  159.1 1.4 copy-start.1
  160.6 1.2 copy-start.3

commit v2 on v0

--- a/solution.py
+++ b/solution.py
@@ -3,6 +3,8 @@
 import jax
 import jax.numpy as jnp
 from jax import lax
+from jax.experimental import pallas as pl
+from jax.experimental.pallas import tpu as pltpu
 from jax.sharding import PartitionSpec as P
 
 HEAD = 64
@@ -246,6 +248,639 @@
     )
 
 
+MESH = pl.DeviceIdType.MESH
+FIRST = (0, 32)
+SECOND = (32, 16)
+
+
+def place_of():
+    me = lax.axis_index("dp")
+    return me // 4, lax.rem(me // 2, 2), lax.rem(me, 2), lax.axis_index("tensor")
+
+
+def flat(z, x, core):
+    return z * 4 + x * 2 + core
+
+
+def greet(z, x, core, side):
+    barrier = pltpu.get_barrier_semaphore()
+
+    def hello(dp, tensor):
+        pl.semaphore_signal(barrier, inc=1, device_id=(dp, tensor), device_id_type=MESH)
+
+    hello(flat(z, 1 - x, core), side)
+    hello(flat(z, x, 1 - core), side)
+    hello(flat(z, x, core), 1 - side)
+
+    @pl.when(z > 0)
+    def _():
+        hello(flat(z - 1, x, core), side)
+
+    @pl.when(z < 3)
+    def _():
+        hello(flat(z + 1, x, core), side)
+
+    edge = jnp.where((z == 0) | (z == 3), 1, 0)
+    pl.semaphore_wait(barrier, 5 - edge)
+
+
+class Sender:
+    def __init__(self, send_sem):
+        self.send_sem = send_sem
+        self.count = 0
+        self.pending = []
+
+    def send(self, source, target, arrive, dp, tensor, cond, like):
+        copy = pltpu.make_async_remote_copy(
+            src_ref=source,
+            dst_ref=target,
+            send_sem=self.send_sem.at[self.count],
+            recv_sem=arrive,
+            device_id=(dp, tensor),
+            device_id_type=MESH,
+        )
+        self.pending.append((self.count, cond, like))
+        self.count += 1
+        copy.start()
+
+    def drain(self):
+        me, side = lax.axis_index("dp"), lax.axis_index("tensor")
+        for index, cond, like in self.pending:
+
+            def finish():
+                pltpu.make_async_remote_copy(
+                    src_ref=like(),
+                    dst_ref=like(),
+                    send_sem=self.send_sem.at[index],
+                    recv_sem=self.send_sem.at[index],
+                    device_id=(me, side),
+                    device_id_type=MESH,
+                ).wait_send()
+
+            if cond is None:
+                finish()
+            else:
+                pl.when(cond())(finish)
+
+
+def rows_at(ref, index, rows=(0, 48)):
+    return ref.at[pl.ds(pl.multiple_of(index * 48 + rows[0], 16), rows[1]), :]
+
+
+class Arrivals:
+    def __init__(self, recv_sem, send_sem, me, side):
+        self.recv_sem, self.send_sem, self.me, self.side = recv_sem, send_sem, me, side
+        self.ids = {}
+
+    def at(self, *name):
+        return self.recv_sem.at[self.ids.setdefault(name, len(self.ids))]
+
+    def wait(self, ref, *name):
+        pltpu.make_async_remote_copy(
+            src_ref=ref,
+            dst_ref=ref,
+            send_sem=self.send_sem.at[0],
+            recv_sem=self.at(*name),
+            device_id=(self.me, self.side),
+            device_id_type=MESH,
+        ).wait_recv()
+
+
+class Gather:
+    def __init__(self, tag, shard, full, sender, arrivals, local, place):
+        self.tag, self.shard, self.full = tag, shard, full
+        self.sender, self.arrivals, self.place = sender, arrivals, place
+        z, x, core, side = place
+        self.copy = pltpu.make_async_copy(shard, rows_at(full, flat(z, x, core)), local)
+
+    def move(self, index, rows, name, dp, cond, own):
+        source = self.shard.at[pl.ds(*rows), :] if own else rows_at(self.full, index, rows)
+        self.sender.send(
+            source,
+            rows_at(self.full, index, rows),
+            self.arrivals.at(self.tag, *name),
+            dp,
+            self.place[3],
+            cond,
+            lambda: rows_at(self.full, 0, rows),
+        )
+
+    def take(self, index, rows, name):
+        self.arrivals.wait(rows_at(self.full, index, rows), self.tag, *name)
+
+    def along(self, way, near, rows, index, other, cond, own):
+        z, x, core, side = self.place
+
+        def both():
+            inside = z < 3 if way > 0 else z > 0
+            return inside if cond is None else inside & cond()
+
+        @pl.when(z < 3 if way > 0 else z > 0)
+        def _():
+            name = ("z", way, near, rows, other)
+            self.move(index, rows, name, flat(z + way, x, core), both, own)
+
+    def across(self, index, rows, distance, cond, own):
+        z, x, core, side = self.place
+        self.move(index, rows, ("x", rows, distance), flat(z, 1 - x, core), cond, own)
+
+    def sibling(self, index, rows, name, cond, own):
+        z, x, core, side = self.place
+        self.move(index, rows, ("c", rows) + name, flat(z, x, 1 - core), cond, own)
+
+    def from_x(self, distance):
+        z, x, core, side = self.place
+
+        def cond():
+            return (z + distance >= 0) & (z + distance <= 3)
+
+        def pass_on():
+            index = flat(z + distance, 1 - x, core)
+            self.take(index, FIRST, ("x", FIRST, distance))
+            self.sibling(index, FIRST, (distance, 1), cond if distance else None, False)
+
+        pl.when(cond())(pass_on) if distance else pass_on()
+
+    def begin(self):
+        z, x, core, side = self.place
+        me = flat(z, x, core)
+        for way in (1, -1):
+            self.along(way, 1, FIRST, me, 0, None, True)
+        self.across(me, SECOND, 0, None, True)
+        self.across(me, FIRST, 0, None, True)
+        for way in (1, -1):
+            self.along(way, 1, SECOND, me, 0, None, True)
+        self.sibling(me, FIRST, (0, 0), None, True)
+        self.sibling(me, SECOND, (0, 0), None, True)
+        self.copy.start()
+
+    def hop(self, near):
+        z, x, core, side = self.place
+        if near == 1:
+            here = flat(z, 1 - x, core)
+            self.take(here, SECOND, ("x", SECOND, 0))
+            for way in (1, -1):
+                self.along(way, 1, SECOND, here, 1, None, False)
+            self.sibling(here, SECOND, (0, 1), None, False)
+        for rows, other in ((FIRST, 0), (SECOND, 0), (SECOND, 1)):
+            for way in (1, -1):
+
+                def cond(way=way, near=near):
+                    return (z - near >= 0) if way > 0 else (z + near <= 3)
+
+                @pl.when(cond())
+                def _():
+                    index = flat(z - way * near, 1 - x if other else x, core)
+                    self.take(index, rows, ("z", way, near, rows, other))
+                    if near < 3:
+                        self.along(way, near + 1, rows, index, other, cond, False)
+                    if rows == FIRST:
+                        self.across(index, rows, -way * near, cond, False)
+                    self.sibling(index, rows, (-way * near, other), cond, False)
+
+        if near == 1:
+            self.from_x(0)
+        else:
+            self.from_x(near - 1)
+            self.from_x(1 - near)
+
+    def finish(self):
+        z, x, core, side = self.place
+        self.from_x(3)
+        self.from_x(-3)
+        for distance in range(-3, 4):
+            for other in (0, 1):
+                for rows in (FIRST, SECOND):
+
+                    def take():
+                        index = flat(z + distance, 1 - x if other else x, 1 - core)
+                        self.take(index, rows, ("c", rows, distance, other))
+
+                    if distance == 0:
+                        take()
+                    else:
+                        pl.when((z + distance >= 0) & (z + distance <= 3))(take)
+        self.copy.wait()
+
+
+class Reduce:
+    def __init__(self, tag, parts, total, buffers, sender, arrivals, place):
+        self.tag, self.parts, self.total = tag, parts, total
+        self.sums, self.from_core, self.got_x, self.up, self.down, self.last_x = buffers
+        self.sender, self.arrivals, self.place = sender, arrivals, place
+
+    def at(self, *name):
+        return self.arrivals.at(self.tag, *name)
+
+    def zq(self, q):
+        z = self.place[0]
+        return jnp.where(z < 2, q, 3 - q)
+
+    def begin(self):
+        z, x, core, side = self.place
+        for q in (3, 2, 1, 0):
+            for other in (1, 0):
+                self.sender.send(
+                    rows_at(self.parts, flat(self.zq(q), 1 - x if other else x, 1 - core)),
+                    self.from_core.at[q * 2 + other],
+                    self.at("c", q, other),
+                    flat(z, x, 1 - core),
+                    side,
+                    None,
+                    lambda: rows_at(self.parts, 0),
+                )
+
+    def spot(self, kind):
+        return ((0, 32), (32, 16), (48, 16))[kind]
+
+    def chain_send(self, way, far, kind, block, cond):
+        z, x, core, side = self.place
+        rows = FIRST if kind == 0 else SECOND
+        buffer = self.up if way > 0 else self.down
+        self.sender.send(
+            self.sums.at[block, pl.ds(*rows), :],
+            buffer.at[far - 1, pl.ds(*self.spot(kind)), :],
+            self.at("z", way, far - 1, kind),
+            flat(z + way, x, core),
+            side,
+            cond,
+            lambda: self.sums.at[0, pl.ds(*rows), :],
+        )
+
+    def add(self, target, left, right, count):
+        @pl.loop(0, count // 16)
+        def _(step):
+            at = pl.ds(pl.multiple_of(step * 16, 16), 16)
+            target[at, :] = left[at, :] + right[at, :]
+
+    def chain_add(self, way, far, kind, block):
+        rows = FIRST if kind == 0 else SECOND
+        got = (self.up if way > 0 else self.down).at[far, pl.ds(*self.spot(kind)), :]
+        self.arrivals.wait(got, self.tag, "z", way, far, kind)
+        here = self.sums.at[block, pl.ds(*rows), :]
+        self.add(here, here, got, rows[1])
+
+    def take_x(self, q):
+        self.arrivals.wait(self.got_x.at[q], self.tag, "x", q)
+        here = self.sums.at[q * 2, pl.ds(*FIRST), :]
+        self.add(here, here, self.got_x.at[q], FIRST[1])
+
+    def edge(self, q, kinds):
+        z = self.place[0]
+        for way in (1, -1):
+
+            def cond(way=way):
+                return (z == 0) if way > 0 else (z == 3)
+
+            @pl.when(cond())
+            def _():
+                for kind in kinds:
+                    self.chain_send(way, q, kind, q * 2 + (1 if kind == 2 else 0), cond)
+
+    def cores(self):
+        z, x, core, side = self.place
+        for q in (3, 2, 1, 0):
+            for other in (1, 0):
+                slot = q * 2 + other
+                self.arrivals.wait(self.from_core.at[slot], self.tag, "c", q, other)
+                mine = rows_at(self.parts, flat(self.zq(q), 1 - x if other else x, core))
+                self.add(self.sums.at[slot], mine, self.from_core.at[slot], 48)
+                if other:
+                    self.sender.send(
+                        self.sums.at[slot, pl.ds(*FIRST), :],
+                        self.got_x.at[q],
+                        self.at("x", q),
+                        flat(z, 1 - x, core),
+                        side,
+                        None,
+                        lambda: self.sums.at[0, pl.ds(*FIRST), :],
+                    )
+            if q > 0:
+                self.edge(q, (1, 2))
+            if q < 3:
+                self.take_x(q + 1)
+                self.edge(q + 1, (0,))
+
+    def middle(self, far):
+        z = self.place[0]
+        if far == 2:
+            self.take_x(0)
+        for kind in (1, 2, 0):
+            for way in (1, -1):
+
+                def cond(way=way, far=far):
+                    return ((z > 0) & (z + far <= 3)) if way > 0 else ((z < 3) & (z - far >= 0))
+
+                @pl.when(cond())
+                def _():
+                    to = z + way * far
+                    q = jnp.where(z < 2, to, 3 - to)
+                    block = q * 2 + (1 if kind == 2 else 0)
+                    self.chain_add(way, far, kind, block)
+                    self.chain_send(way, far, kind, block, cond)
+
+    def arrive(self):
+        z, x, core, side = self.place
+        own_q = jnp.where(z < 2, z, 3 - z)
+        for kind in (2, 1, 0):
+            block = own_q * 2 + (1 if kind == 2 else 0)
+            for way in (1, -1):
+
+                @pl.when((z > 0) if way > 0 else (z < 3))
+                def _():
+                    self.chain_add(way, 0, kind, block)
+
+            if kind == 2:
+                self.sender.send(
+                    self.sums.at[block, pl.ds(*SECOND), :],
+                    self.last_x,
+                    self.at("lx"),
+                    flat(z, 1 - x, core),
+                    side,
+                    None,
+                    lambda: self.last_x,
+                )
+        own = own_q * 2
+
+        @pl.loop(0, 2)
+        def _(step):
+            at = pl.ds(pl.multiple_of(step * 16, 16), 16)
+            self.total[at, :] = self.sums[own, at, :].astype(jnp.float32)
+
+        self.arrivals.wait(self.last_x, self.tag, "lx")
+        ours = self.sums[own, 32:48, :].astype(jnp.float32)
+        self.total[32:48, :] = ours + self.last_x[...].astype(jnp.float32)
+
+
+def turn(tile, wave, sign):
+    cos, sin_low, sin_high = wave
+    ahead = pltpu.roll(tile, 128 - ROT // 2, 1)
+    behind = pltpu.roll(tile, ROT // 2, 1)
+    return tile * cos[...] + sign * (behind * sin_high[...] - ahead * sin_low[...])
+
+
+def layer_kernel(*refs):
+    (shard0, shard1, shard2, tok, cot, cos, sin_low, sin_high, open_mask) = refs[:9]
+    output, grad_tokens, total0, total1, total2 = refs[9:14]
+    (
+        w0, w1, w2, tok_all, cot_all, cot_t, xhat, params, n1, n2, n1_t, n2_t,
+        qs, ks, vs, ags, attended, pg, branch, n1g, n2g, norm_t,
+        parts0, parts1, parts2, to_peer, from_peer, norm_send, norm_recv,
+    ) = refs[14:43]
+    buffers = [refs[43 + 6 * i : 49 + 6 * i] for i in range(3)]
+    send_sem, recv_sem, local_sem = refs[61:]
+    place = place_of()
+    z, x, core, side = place
+    me = flat(z, x, core)
+    sender = Sender(send_sem)
+    arrivals = Arrivals(recv_sem, send_sem, me, side)
+    gathers = [
+        Gather(("g", i), shard, full, sender, arrivals, local_sem.at[i], place)
+        for i, (shard, full) in enumerate(((shard0, w0), (shard1, w1), (shard2, w2)))
+    ]
+    reduces = [
+        Reduce(("r", i), parts, total, buffers[i], sender, arrivals, place)
+        for i, (parts, total) in enumerate(
+            ((parts0, total0), (parts1, total1), (parts2, total2))
+        )
+    ]
+    low, f32 = jnp.bfloat16, jnp.float32
+    half = tok.shape[0]
+    mine, theirs = pl.ds(side * half, half), pl.ds((1 - side) * half, half)
+    wide = qs.shape[1]
+    scale = 1.0 / math.sqrt(HEAD)
+    wave = (cos, sin_low, sin_high)
+
+    greet(z, x, core, side)
+    gathers[0].begin()
+    sender.send(tok, tok_all.at[mine, :], arrivals.at("tok"), me, 1 - side, None, lambda: tok)
+    sender.send(cot, cot_all.at[mine, :], arrivals.at("cot"), me, 1 - side, None, lambda: cot)
+    tok_all[mine, :] = tok[...]
+    cot_all[mine, :] = cot[...]
+    arrivals.wait(tok_all.at[theirs, :], "tok")
+    arrivals.wait(cot_all.at[theirs, :], "cot")
+    xhat[...] = plain_norm(tok_all[...].astype(f32))[0]
+    cot_t[...] = cot_all[...].astype(f32).T.astype(low)
+    gathers[0].hop(1)
+    gathers[1].begin()
+    gathers[0].hop(2)
+    gathers[0].hop(3)
+    gathers[1].hop(1)
+    gathers[0].finish()
+    gathers[2].begin()
+
+    params[...] = w0[:, 4 * wide :].astype(f32).T
+    for at, norm, norm_tr in ((0, n1, n1_t), (2, n2, n2_t)):
+        value = xhat[...] * params[at : at + 1, :] + params[at + 1 : at + 2, :]
+        norm[...] = value.astype(low)
+        norm_tr[...] = value.T.astype(low)
+    for at, target in enumerate((qs, ks, vs)):
+        tile = contract(n1[...], w0[:, at * wide : (at + 1) * wide], 1, 0)
+        for j in range(wide // 128):
+            piece = tile[:, j * 128 : (j + 1) * 128]
+            if at < 2:
+                piece = turn(piece, wave, 1.0)
+            target[:, j * 128 : (j + 1) * 128] = piece.astype(low)
+    ags[...] = contract(cot_all[...], w0[:, 3 * wide : 4 * wide], 1, 0).astype(low)
+    gathers[1].hop(2)
+
+    def pair(j):
+        sl = slice(j * 128, (j + 1) * 128)
+        q, k, v, ag = qs[:, sl], ks[:, sl], vs[:, sl], ags[:, sl]
+        left = lax.broadcasted_iota(jnp.int32, q.shape, 1) < HEAD
+        both = []
+        for head in (0, 1):
+            keep = jnp.where(left, 1.0 - head, 1.0 * head).astype(low)
+            scores = contract(q * keep, k, 1, 1) * scale
+            scores = jnp.where(open_mask[...] > 0.5, scores, masked_score)
+            exponent = jnp.exp(scores - jnp.max(scores, axis=-1, keepdims=True))
+            prob = exponent / jnp.sum(exponent, axis=-1, keepdims=True)
+            prob_low = prob.astype(low)
+            prob_grad = contract(ag * keep, v, 1, 1)
+            row_dot = jnp.sum(prob * prob_grad, axis=-1, keepdims=True)
+            score_grad = (prob * (prob_grad - row_dot)).astype(low)
+            both.append(
+                (
+                    contract(prob_low, v, 1, 0),
+                    contract(score_grad, k, 1, 0) * scale,
+                    contract(score_grad, q, 0, 0) * scale,
+                    contract(prob_low, ag, 0, 0),
+                )
+            )
+        att, dq, dk, dv = (jnp.where(left, a, b) for a, b in zip(*both))
+        attended[:, sl] = att.astype(low)
+        pg[:, j * 128 : (j + 1) * 128] = turn(dq, wave, -1.0).astype(low)
+        pg[:, wide + j * 128 : wide + (j + 1) * 128] = turn(dk, wave, -1.0).astype(low)
+        pg[:, 2 * wide + j * 128 : 2 * wide + (j + 1) * 128] = dv.astype(low)
+
+    pair(0)
+    gathers[1].hop(3)
+    gathers[2].hop(1)
+    pair(1)
+    gathers[1].finish()
+    pair(2)
+    gathers[2].hop(2)
+    for at in range(3):
+        sl = slice(at * wide, (at + 1) * wide)
+        parts0[:, sl] = jnp.dot(n1_t[...], pg[:, sl], preferred_element_type=f32).astype(low)
+    parts0[:, 3 * wide :] = jnp.dot(
+        cot_t[...], attended[...], preferred_element_type=f32
+    ).astype(low)
+    reduces[0].begin()
+    gathers[2].hop(3)
+    n1g[...] = contract(pg[...], w0[:, : 3 * wide], 1, 1)
+    branch[...] = contract(attended[...], w0[:, 3 * wide : 4 * wide], 1, 1)
+    n2g[...] = jnp.zeros_like(n2g)
+
+    def hidden_part(w, parts):
+        size = w.shape[1] // 2
+
+        @pl.loop(0, size // 256)
+        def _(step):
+            at = pl.ds(pl.multiple_of(step * 256, 256), 256)
+            at_down = pl.ds(pl.multiple_of(size + step * 256, 256), 256)
+            hidden = contract(n2[...], w[:, at], 1, 0)
+            cdf = 0.5 * (1.0 + lax.erf(hidden * math.sqrt(0.5)))
+            bell = jnp.exp(-0.5 * hidden * hidden) * (1.0 / math.sqrt(2.0 * math.pi))
+            act = (hidden * cdf).astype(low)
+            pre = ((cdf + hidden * bell) * contract(cot_all[...], w[:, at_down], 1, 0)).astype(low)
+            parts[:, at] = jnp.dot(n2_t[...], pre, preferred_element_type=f32).astype(low)
+            parts[:, at_down] = jnp.dot(cot_t[...], act, preferred_element_type=f32).astype(low)
+            branch[...] += contract(act, w[:, at_down], 1, 1)
+            n2g[...] += contract(pre, w[:, at], 1, 1)
+
+    hidden_part(w1, parts1)
+    reduces[0].cores()
+    reduces[1].begin()
+    gathers[2].finish()
+    hidden_part(w2, parts2)
+    norm_t[...] = jnp.zeros_like(norm_t)
+    for at, grad in ((0, n1g), (2, n2g)):
+        norm_t[at : at + 1, :] = jnp.sum(grad[...] * xhat[...], axis=0, keepdims=True)
+        norm_t[at + 1 : at + 2, :] = jnp.sum(grad[...], axis=0, keepdims=True)
+    parts2[:, w2.shape[1] :] = norm_t[...].T.astype(low)
+    reduces[2].begin()
+    for at, ref in enumerate((branch, n1g, n2g)):
+        to_peer[at] = ref[theirs, :].astype(low)
+    sender.send(to_peer, from_peer, arrivals.at("y"), me, 1 - side, None, lambda: to_peer)
+    reduces[0].middle(2)
+    reduces[1].cores()
+    reduces[0].middle(1)
+    reduces[0].arrive()
+    reduces[1].middle(2)
+    reduces[2].cores()
+    reduces[1].middle(1)
+    reduces[1].arrive()
+    reduces[2].middle(2)
+    arrivals.wait(from_peer, "y")
+    tok_f = tok[...].astype(f32)
+    output[...] = (tok_f + (branch[mine, :] + from_peer[0].astype(f32))).astype(low)
+    one, two = (ref[mine, :] + from_peer[at].astype(f32) for at, ref in ((1, n1g), (2, n2g)))
+    hat, inverse = plain_norm(tok_f)
+    grad = one * params[0:1, :] + two * params[2:3, :]
+    grad_tokens[...] = cot[...].astype(f32) + inverse * (
+        grad
+        - jnp.mean(grad, axis=-1, keepdims=True)
+        - hat * jnp.mean(grad * hat, axis=-1, keepdims=True)
+    )
+    reduces[2].middle(1)
+    reduces[2].arrive()
+    norm_send[...] = total2[:, w2.shape[1] :]
+    sender.send(norm_send, norm_recv, arrivals.at("n"), me, 1 - side, None, lambda: norm_send)
+    arrivals.wait(norm_recv, "n")
+    total2[:, w2.shape[1] :] = norm_send[...] + norm_recv[...]
+    sender.drain()
+
+
+def layer_call(shards, tok, cot, waves, open_mask, heads):
+    rows, d = 2 * tok.shape[0], tok.shape[1]
+    low, f32 = jnp.bfloat16, jnp.float32
+    vmem = pl.BlockSpec(memory_space=pltpu.VMEM)
+    wide = heads * HEAD
+    widths = [4 * wide, shards[1].shape[1], shards[2].shape[1] + 128]
+    out_shape = [jax.ShapeDtypeStruct(tok.shape, low), jax.ShapeDtypeStruct(tok.shape, f32)]
+    out_shape += [jax.ShapeDtypeStruct((48, w), f32) for w in widths]
+    scratch = [pltpu.VMEM((d, s.shape[1]), low) for s in shards]
+    scratch += [pltpu.VMEM((rows, d), low)] * 2
+    scratch += [pltpu.VMEM((d, rows), low), pltpu.VMEM((rows, d), f32), pltpu.VMEM((128, d), f32)]
+    scratch += [pltpu.VMEM((rows, d), low)] * 2 + [pltpu.VMEM((d, rows), low)] * 2
+    scratch += [pltpu.VMEM((rows, wide), low)] * 5
+    scratch += [pltpu.VMEM((rows, 3 * wide), low)]
+    scratch += [pltpu.VMEM((rows, d), f32)] * 3 + [pltpu.VMEM((128, d), f32)]
+    scratch += [pltpu.VMEM((d, w), low) for w in widths]
+    scratch += [pltpu.VMEM((3, rows // 2, d), low)] * 2
+    scratch += [pltpu.VMEM((48, 128), f32)] * 2
+    for w in widths:
+        scratch += [pltpu.VMEM((8, 48, w), low)] * 2
+        scratch += [pltpu.VMEM((4, FIRST[1], w), low)]
+        scratch += [pltpu.VMEM((3, 64, w), low)] * 2
+        scratch += [pltpu.VMEM((SECOND[1], w), low)]
+    scratch += [pltpu.SemaphoreType.DMA((384,))] * 2 + [pltpu.SemaphoreType.DMA((3,))]
+    return pl.pallas_call(
+        layer_kernel,
+        out_shape=out_shape,
+        in_specs=[vmem] * 9,
+        out_specs=[vmem] * 5,
+        scratch_shapes=scratch,
+        compiler_params=pltpu.CompilerParams(
+            collective_id=0, has_side_effects=True, vmem_limit_bytes=58 * 1024 * 1024
+        ),
+        name="layer",
+    )(*shards, tok, cot, *waves, open_mask)
+
+
+def plain_norm(values):
+    center = values - jnp.mean(values, axis=-1, keepdims=True)
+    spread = jnp.mean(center * center, axis=-1, keepdims=True)
+    inverse = lax.rsqrt(spread + norm_eps)
+    return center * inverse, inverse
+
+
+def line_device(
+    tokens, ln1_gain, ln1_bias, ln2_gain, ln2_bias, w_qkv, w_out, w_up, w_down, grad_out, lengths
+):
+    heads = w_qkv.shape[1] // (3 * HEAD)
+    own = w_qkv.shape[0]
+    wide = heads * HEAD
+    split = w_up.shape[1] // 2
+    norm_params = jnp.stack([ln1_gain, ln1_bias, ln2_gain, ln2_bias], axis=1)
+    qkv = w_qkv.reshape(own, heads, 3, HEAD).transpose(0, 2, 1, 3).reshape(own, 3 * wide)
+    down = w_down.T
+    shards = (
+        jnp.concatenate([qkv, w_out.T, jnp.pad(norm_params, ((0, 0), (0, 124)))], axis=1),
+        jnp.concatenate([w_up[:, :split], down[:, :split]], axis=1),
+        jnp.concatenate([w_up[:, split:], down[:, split:]], axis=1),
+    )
+    rows = 2 * tokens.shape[0]
+    segment, positions, places = doc_layout(lengths[0], rows)
+    wave_cos, wave_sin = rope_tables(positions)
+    rest = HEAD - ROT
+    none = jnp.zeros_like(wave_sin)
+    cos = jnp.concatenate([wave_cos, wave_cos, jnp.ones((rows, rest), jnp.float32)], axis=1)
+    blank = jnp.zeros((rows, rest), jnp.float32)
+    sin_low = jnp.concatenate([wave_sin, none, blank], axis=1)
+    sin_high = jnp.concatenate([none, wave_sin, blank], axis=1)
+    waves = [jnp.concatenate([table, table], axis=1) for table in (cos, sin_low, sin_high)]
+    allowed = (segment[:, None] == segment[None, :]) & (places[:, None] >= places[None, :])
+    output, grad_tokens, total0, total1, total2 = layer_call(
+        shards, tokens, grad_out, waves, allowed.astype(jnp.float32), heads
+    )
+    qkv_grad = total0[:, : 3 * wide].reshape(own, 3, heads, HEAD).transpose(0, 2, 1, 3)
+    norm_total = total2[:, 2 * split : 2 * split + 4].T
+    return (
+        output,
+        grad_tokens,
+        norm_total[0],
+        norm_total[1],
+        norm_total[2],
+        norm_total[3],
+        qkv_grad.reshape(own, 3 * wide),
+        total0[:, 3 * wide :].T,
+        jnp.concatenate([total1[:, :split], total2[:, :split]], axis=1),
+        jnp.concatenate([total1[:, split:], total2[:, split : 2 * split]], axis=1).T,
+    )
+
+
 def solution(mesh):
     placed = (
         P(("dp", "tensor"), None),
@@ -260,8 +895,9 @@
         P(("dp", "tensor"), None),
         P("dp", None),
     )
+    body = line_device if mesh.shape["dp"] == 16 and mesh.shape["tensor"] == 2 else per_device
     return jax.shard_map(
-        per_device,
+        body,
         mesh=mesh,
         in_specs=placed,
         out_specs=(

time: 516 us -> 142 us (0.28)
  waiting for transfers between devices: 279 us -> 0 us
  Pallas kernels: 0 us -> 121 us
  blocking collectives: 70 us -> 0 us
  local copies, waits for them, and re-layouts: 55.2 us -> 12.8 us
  matrix products: 31 us -> 0 us
  starting transfers between devices: 29.7 us -> 0 us
  other arithmetic: 32.1 us -> 4.59 us
  between operations: 14.7 us -> 0.79 us
    all_to_all x5 -> x0, waiting for transfers between devices: 197 us -> none  [the longest x1 88.5 us: per_device(): lax.all_to_all(grad_down_t[None], 'dp', split_axis=1, concat_axis=0, tile...]
    pallas_call x0 -> x1, Pallas kernels: none -> 121 us  [layer_call(): pl.pallas_call(layer_kernel, out_shape=out_shape, in_specs=[vmem] * 9, ou...]
    all_gather x5 -> x0, blocking collectives: 61.5 us -> none  [the longest x1 19.8 us: per_device(): lax.all_gather(w_out, 'dp', axis=1, tiled=True)]
    all_gather x3 -> x0, waiting for transfers between devices: 49.4 us -> none  [the longest x1 40.8 us: per_device(): lax.all_gather(w_down, 'dp', axis=1, tiled=True)]
    dot_general x18 -> x0, matrix products: 31 us -> none  [the longest x8 18.8 us: contract(): lax.dot_general(first_op, second_op, (((first_dim,), (second_dim,)), ((),...]
    reduce_scatter x3 -> x0, waiting for transfers between devices: 30.9 us -> none  [the longest x1 19.2 us: per_device(): lax.psum_scatter(norm_two_grad, 'tensor', scatter_dimension=0, tiled=True)]
    broadcast_in_dim x5 -> x3, local copies, waits for them, and re-layouts: 30.1 us -> 0.03 us  [the longest x1 0.01 us: line_device(): jnp.ones((rows, rest), jnp.float32)]
    all_to_all x5 -> x0, starting transfers between devices: 29.4 us -> none  [the longest x1 6.55 us: per_device(): lax.all_to_all(grad_up[None], 'dp', split_axis=1, concat_axis=0, tiled=True)]
  transfers between devices with their start and end apart: 11 -> 0, of which waited for: 8 -> 0; matrix products, arithmetic and copies ran while one was open for 20% -> 0% of each run, Pallas kernels for 0% -> 0%
where the time goes in v2:
time: 142 us; the launch traced here: 139 us
  Pallas kernels  121 us (85%)
  local copies, waits for them, and re-layouts  12.8 us (9%)
  other arithmetic  4.59 us (3%)
    pallas_call x1, Pallas kernels, layer_call(): pl.pallas_call(layer_kernel, out_shape=out_shape, in_specs=[vmem] * 9, ou...  121 us
    unnamed x26, local copies, waits for them, and re-layouts  4.11 us

profile of v2, /device:TPU:8, one launch (start us, length us, event | category | flops | bytes accessed | tf_op | source)
XLA Modules:
  0.0 138.9 jit_solution(7401739654788647524)
XLA Ops:
  0.6 0.0 copy-start.11
  0.7 0.6 copy-done.11
  1.3 0.2 reduce-window.4
  1.5 0.1 convert_reduce_fusion
  1.6 0.1 select_reduce_fusion
  1.7 0.0 copy-start.7
  1.7 0.0 copy-start.8
  1.7 0.0 copy-start.9
  1.7 0.0 copy-start.10
  1.7 0.6 copy-done.7
  2.3 0.0 copy-done.8
  2.3 0.0 copy-done.9
  2.4 0.0 copy-done.10
  2.4 0.1 copy.37
  2.5 0.0 copy-start.4
  2.5 1.0 fusion.7
  3.5 0.0 copy-done.4
  3.5 0.7 pad_maximum_fusion.1
  4.2 0.5 multiply_sine_fusion
  4.8 0.9 concatenate.33.refs_5_
  5.7 0.9 concatenate.35.refs_7_
  6.6 0.9 concatenate.34.refs_6_
  7.5 0.0 copy-start.5
  7.5 0.8 fusion.2.refs_8_
  8.3 0.1 copy-done.5
  8.4 0.2 reshape.56
  8.6 0.1 copy.36
  8.6 0.0 copy-start.6
  8.6 0.2 reshape.57
  8.9 0.5 copy-done.6
  9.4 0.7 fusion.3.refs_0_
  10.1 120.7 %layer.1 = (bf16[128,768]{1,0:T(8,128)(2,1)}, f32[128,768]{1,0:T(8,128)}, f32[48,1536]{1,0:T(8,128)}, f32[48,1536]{1,0:T(8,128)}, f32[48,1664]{1,0:T(8,128)}) custom-call(bf16[48,1664]{1,0:T(8,128)(2,1)} %fusion.3.refs_0_, bf16[48,1536]{1,0:T(8,128)(2,1)} %get-tuple-element.34.refs_1_, bf16[48,1536]{1,0:T(8,128)(2,1)} %get-tuple-element.35.refs_2_, ...), custom_call_target="tpu_custom_call" | custom-call | tf_op jit(solution)/shard_map/layer/pallas_call | solution.py:819
  130.8 0.7 slice_bitcast_fusion.1
  131.5 1.0 fusion.5
  132.6 0.7 slice_reduce_fusion
  133.3 0.0 copy-done.1
  133.3 0.6 slice_bitcast_fusion
  134.0 0.3 copy-done.2
  134.3 0.7 maximum_bitcast_fusion
  135.1 0.7 pad_maximum_fusion
  135.8 0.1 reshape.60
  135.9 0.2 copy.38
  136.1 0.0 copy-start.3
  136.1 1.0 reshape.61
  137.1 0.0 copy-done.3
  137.1 0.7 copy.41
  137.8 0.4 copy-done
  138.1 0.7 copy.42
  (13 shorter events, 0.1 us)
Async XLA Ops:
  0.6 0.7 copy-start.11
  1.7 0.7 copy-start.7
  1.7 0.7 copy-start.8
  1.7 0.7 copy-start.9
  1.7 0.7 copy-start.10
  2.5 1.0 copy-start.4
  7.5 0.9 copy-start.5
  8.6 0.8 copy-start.6
  131.5 1.8 %copy-start.1 = (f32[48,1536]{1,0:T(8,128)S(1)}, f32[48,1536]{1,0:T(8,128)}, u32[]{:S(2)}) copy-start(f32[48,1536]{1,0:T(8,128)} %get-tuple-element.18) | copy-start | bytes 884740
  133.3 1.0 copy-start.2
  136.1 1.0 copy-start.3
  137.1 1.1 copy-start

commit v3 on v2

--- a/solution.py
+++ b/solution.py
@@ -1,3 +1,4 @@
+import functools
 import math
 
 import jax
@@ -251,6 +252,7 @@
 MESH = pl.DeviceIdType.MESH
 FIRST = (0, 32)
 SECOND = (32, 16)
+WHOLE = (0, 48)
 
 
 def place_of():
@@ -397,32 +399,28 @@
         def pass_on():
             index = flat(z + distance, 1 - x, core)
             self.take(index, FIRST, ("x", FIRST, distance))
-            self.sibling(index, FIRST, (distance, 1), cond if distance else None, False)
-
-        pl.when(cond())(pass_on) if distance else pass_on()
+            self.sibling(index, WHOLE, (distance, 1), cond, False)
+
+        pl.when(cond())(pass_on)
 
     def begin(self):
         z, x, core, side = self.place
         me = flat(z, x, core)
+        self.across(me, WHOLE, 0, None, True)
         for way in (1, -1):
-            self.along(way, 1, FIRST, me, 0, None, True)
-        self.across(me, SECOND, 0, None, True)
-        self.across(me, FIRST, 0, None, True)
-        for way in (1, -1):
-            self.along(way, 1, SECOND, me, 0, None, True)
-        self.sibling(me, FIRST, (0, 0), None, True)
-        self.sibling(me, SECOND, (0, 0), None, True)
+            self.along(way, 1, WHOLE, me, 0, None, True)
+        self.sibling(me, WHOLE, (0, 0), None, True)
         self.copy.start()
 
     def hop(self, near):
         z, x, core, side = self.place
         if near == 1:
             here = flat(z, 1 - x, core)
-            self.take(here, SECOND, ("x", SECOND, 0))
+            self.take(here, WHOLE, ("x", WHOLE, 0))
             for way in (1, -1):
                 self.along(way, 1, SECOND, here, 1, None, False)
-            self.sibling(here, SECOND, (0, 1), None, False)
-        for rows, other in ((FIRST, 0), (SECOND, 0), (SECOND, 1)):
+            self.sibling(here, WHOLE, (0, 1), None, False)
+        for rows, other in ((WHOLE, 0), (SECOND, 1)):
             for way in (1, -1):
 
                 def cond(way=way, near=near):
@@ -434,13 +432,11 @@
                     self.take(index, rows, ("z", way, near, rows, other))
                     if near < 3:
                         self.along(way, near + 1, rows, index, other, cond, False)
-                    if rows == FIRST:
-                        self.across(index, rows, -way * near, cond, False)
-                    self.sibling(index, rows, (-way * near, other), cond, False)
-
-        if near == 1:
-            self.from_x(0)
-        else:
+                    if rows == WHOLE:
+                        self.across(index, FIRST, -way * near, cond, False)
+                        self.sibling(index, WHOLE, (-way * near, other), cond, False)
+
+        if near > 1:
             self.from_x(near - 1)
             self.from_x(1 - near)
 
@@ -450,16 +446,15 @@
         self.from_x(-3)
         for distance in range(-3, 4):
             for other in (0, 1):
-                for rows in (FIRST, SECOND):
-
-                    def take():
-                        index = flat(z + distance, 1 - x if other else x, 1 - core)
-                        self.take(index, rows, ("c", rows, distance, other))
-
-                    if distance == 0:
-                        take()
-                    else:
-                        pl.when((z + distance >= 0) & (z + distance <= 3))(take)
+
+                def take():
+                    index = flat(z + distance, 1 - x if other else x, 1 - core)
+                    self.take(index, WHOLE, ("c", WHOLE, distance, other))
+
+                if distance == 0:
+                    take()
+                else:
+                    pl.when((z + distance >= 0) & (z + distance <= 3))(take)
         self.copy.wait()
 
 
@@ -491,11 +486,11 @@
                 )
 
     def spot(self, kind):
-        return ((0, 32), (32, 16), (48, 16))[kind]
+        return (48, 16) if kind else (0, 48)
 
     def chain_send(self, way, far, kind, block, cond):
         z, x, core, side = self.place
-        rows = FIRST if kind == 0 else SECOND
+        rows = WHOLE if kind == 0 else SECOND
         buffer = self.up if way > 0 else self.down
         self.sender.send(
             self.sums.at[block, pl.ds(*rows), :],
@@ -514,7 +509,7 @@
             target[at, :] = left[at, :] + right[at, :]
 
     def chain_add(self, way, far, kind, block):
-        rows = FIRST if kind == 0 else SECOND
+        rows = WHOLE if kind == 0 else SECOND
         got = (self.up if way > 0 else self.down).at[far, pl.ds(*self.spot(kind)), :]
         self.arrivals.wait(got, self.tag, "z", way, far, kind)
         here = self.sums.at[block, pl.ds(*rows), :]
@@ -556,7 +551,7 @@
                         lambda: self.sums.at[0, pl.ds(*FIRST), :],
                     )
             if q > 0:
-                self.edge(q, (1, 2))
+                self.edge(q, (2,))
             if q < 3:
                 self.take_x(q + 1)
                 self.edge(q + 1, (0,))
@@ -565,7 +560,7 @@
         z = self.place[0]
         if far == 2:
             self.take_x(0)
-        for kind in (1, 2, 0):
+        for kind in (2, 0):
             for way in (1, -1):
 
                 def cond(way=way, far=far):
@@ -582,7 +577,7 @@
     def arrive(self):
         z, x, core, side = self.place
         own_q = jnp.where(z < 2, z, 3 - z)
-        for kind in (2, 1, 0):
+        for kind in (2, 0):
             block = own_q * 2 + (1 if kind == 2 else 0)
             for way in (1, -1):
 
@@ -619,16 +614,29 @@
     return tile * cos[...] + sign * (behind * sin_high[...] - ahead * sin_low[...])
 
 
+ORDER = (
+    "g0b ts g1b th",
+    "g01 g11 g02 g12",
+    "g03 g0f na pr",
+    "g13 p0 p1 p2",
+    "ag r0b g1f ab",
+    "r0c h1 ns r1b",
+    "rs r02 r01 r0a",
+    "r1c r12 ro r11",
+    "r1a no",
+)
+
+
 def layer_kernel(*refs):
-    (shard0, shard1, shard2, tok, cot, cos, sin_low, sin_high, open_mask) = refs[:9]
-    output, grad_tokens, total0, total1, total2 = refs[9:14]
+    (shard0, shard1, tok, cot, wave_table, open_mask) = refs[:6]
+    output, grad_tokens, total0, total1 = refs[6:10]
     (
-        w0, w1, w2, tok_all, cot_all, cot_t, xhat, params, n1, n2, n1_t, n2_t,
+        w0, w1, tok_all, cot_all, cot_t, xhat, params, n1, n2, n1_t, n2_t,
         qs, ks, vs, ags, attended, pg, branch, n1g, n2g, norm_t,
-        parts0, parts1, parts2, to_peer, from_peer, norm_send, norm_recv,
-    ) = refs[14:43]
-    buffers = [refs[43 + 6 * i : 49 + 6 * i] for i in range(3)]
-    send_sem, recv_sem, local_sem = refs[61:]
+        parts0, parts1, to_peer, from_peer, norm_send, norm_recv,
+    ) = refs[10:37]
+    buffers = [refs[37 + 6 * i : 43 + 6 * i] for i in range(2)]
+    send_sem, recv_sem, local_sem = refs[49:]
     place = place_of()
     z, x, core, side = place
     me = flat(z, x, core)
@@ -636,12 +644,12 @@
     arrivals = Arrivals(recv_sem, send_sem, me, side)
     gathers = [
         Gather(("g", i), shard, full, sender, arrivals, local_sem.at[i], place)
-        for i, (shard, full) in enumerate(((shard0, w0), (shard1, w1), (shard2, w2)))
+        for i, (shard, full) in enumerate(((shard0, w0), (shard1, w1)))
     ]
     reduces = [
         Reduce(("r", i), parts, total, buffers[i], sender, arrivals, place)
         for i, (parts, total) in enumerate(
-            ((parts0, total0), (parts1, total1), (parts2, total2))
+            ((parts0, total0), (parts1, total1))
         )
     ]
     low, f32 = jnp.bfloat16, jnp.float32
@@ -649,40 +657,38 @@
     mine, theirs = pl.ds(side * half, half), pl.ds((1 - side) * half, half)
     wide = qs.shape[1]
     scale = 1.0 / math.sqrt(HEAD)
-    wave = (cos, sin_low, sin_high)
-
-    greet(z, x, core, side)
-    gathers[0].begin()
-    sender.send(tok, tok_all.at[mine, :], arrivals.at("tok"), me, 1 - side, None, lambda: tok)
-    sender.send(cot, cot_all.at[mine, :], arrivals.at("cot"), me, 1 - side, None, lambda: cot)
-    tok_all[mine, :] = tok[...]
-    cot_all[mine, :] = cot[...]
-    arrivals.wait(tok_all.at[theirs, :], "tok")
-    arrivals.wait(cot_all.at[theirs, :], "cot")
-    xhat[...] = plain_norm(tok_all[...].astype(f32))[0]
-    cot_t[...] = cot_all[...].astype(f32).T.astype(low)
-    gathers[0].hop(1)
-    gathers[1].begin()
-    gathers[0].hop(2)
-    gathers[0].hop(3)
-    gathers[1].hop(1)
-    gathers[0].finish()
-    gathers[2].begin()
-
-    params[...] = w0[:, 4 * wide :].astype(f32).T
-    for at, norm, norm_tr in ((0, n1, n1_t), (2, n2, n2_t)):
-        value = xhat[...] * params[at : at + 1, :] + params[at + 1 : at + 2, :]
-        norm[...] = value.astype(low)
-        norm_tr[...] = value.T.astype(low)
-    for at, target in enumerate((qs, ks, vs)):
-        tile = contract(n1[...], w0[:, at * wide : (at + 1) * wide], 1, 0)
-        for j in range(wide // 128):
-            piece = tile[:, j * 128 : (j + 1) * 128]
-            if at < 2:
-                piece = turn(piece, wave, 1.0)
-            target[:, j * 128 : (j + 1) * 128] = piece.astype(low)
-    ags[...] = contract(cot_all[...], w0[:, 3 * wide : 4 * wide], 1, 0).astype(low)
-    gathers[1].hop(2)
+    wave = [wave_table.at[:, 128 * i : 128 * (i + 1)] for i in range(3)]
+
+    def tokens_sent():
+        sender.send(tok, tok_all.at[mine, :], arrivals.at("tok"), me, 1 - side, None, lambda: tok)
+        sender.send(cot, cot_all.at[mine, :], arrivals.at("cot"), me, 1 - side, None, lambda: cot)
+        tok_all[mine, :] = tok[...]
+        cot_all[mine, :] = cot[...]
+
+    def tokens_here():
+        arrivals.wait(tok_all.at[theirs, :], "tok")
+        arrivals.wait(cot_all.at[theirs, :], "cot")
+        xhat[...] = plain_norm(tok_all[...].astype(f32))[0]
+        cot_t[...] = cot_all[...].astype(f32).T.astype(low)
+        n2g[...] = jnp.zeros_like(n2g)
+        norm_t[...] = jnp.zeros_like(norm_t)
+
+    def norms_applied():
+        params[...] = w0[:, 4 * wide :].astype(f32).T
+        for at, norm, norm_tr in ((0, n1, n1_t), (2, n2, n2_t)):
+            value = xhat[...] * params[at : at + 1, :] + params[at + 1 : at + 2, :]
+            norm[...] = value.astype(low)
+            norm_tr[...] = value.T.astype(low)
+
+    def projections():
+        for at, target in enumerate((qs, ks, vs)):
+            tile = contract(n1[...], w0[:, at * wide : (at + 1) * wide], 1, 0)
+            for j in range(wide // 128):
+                piece = tile[:, j * 128 : (j + 1) * 128]
+                if at < 2:
+                    piece = turn(piece, wave, 1.0)
+                target[:, j * 128 : (j + 1) * 128] = piece.astype(low)
+        ags[...] = contract(cot_all[...], w0[:, 3 * wide : 4 * wide], 1, 0).astype(low)
 
     def pair(j):
         sl = slice(j * 128, (j + 1) * 128)
@@ -713,24 +719,17 @@
         pg[:, wide + j * 128 : wide + (j + 1) * 128] = turn(dk, wave, -1.0).astype(low)
         pg[:, 2 * wide + j * 128 : 2 * wide + (j + 1) * 128] = dv.astype(low)
 
-    pair(0)
-    gathers[1].hop(3)
-    gathers[2].hop(1)
-    pair(1)
-    gathers[1].finish()
-    pair(2)
-    gathers[2].hop(2)
-    for at in range(3):
-        sl = slice(at * wide, (at + 1) * wide)
-        parts0[:, sl] = jnp.dot(n1_t[...], pg[:, sl], preferred_element_type=f32).astype(low)
-    parts0[:, 3 * wide :] = jnp.dot(
-        cot_t[...], attended[...], preferred_element_type=f32
-    ).astype(low)
-    reduces[0].begin()
-    gathers[2].hop(3)
-    n1g[...] = contract(pg[...], w0[:, : 3 * wide], 1, 1)
-    branch[...] = contract(attended[...], w0[:, 3 * wide : 4 * wide], 1, 1)
-    n2g[...] = jnp.zeros_like(n2g)
+    def attention_grads():
+        for at in range(3):
+            sl = slice(at * wide, (at + 1) * wide)
+            parts0[:, sl] = jnp.dot(n1_t[...], pg[:, sl], preferred_element_type=f32).astype(low)
+        parts0[:, 3 * wide :] = jnp.dot(
+            cot_t[...], attended[...], preferred_element_type=f32
+        ).astype(low)
+
+    def attention_back():
+        n1g[...] = contract(pg[...], w0[:, : 3 * wide], 1, 1)
+        branch[...] = contract(attended[...], w0[:, 3 * wide : 4 * wide], 1, 1)
 
     def hidden_part(w, parts):
         size = w.shape[1] // 2
@@ -749,46 +748,56 @@
             branch[...] += contract(act, w[:, at_down], 1, 1)
             n2g[...] += contract(pre, w[:, at], 1, 1)
 
-    hidden_part(w1, parts1)
-    reduces[0].cores()
-    reduces[1].begin()
-    gathers[2].finish()
-    hidden_part(w2, parts2)
-    norm_t[...] = jnp.zeros_like(norm_t)
-    for at, grad in ((0, n1g), (2, n2g)):
-        norm_t[at : at + 1, :] = jnp.sum(grad[...] * xhat[...], axis=0, keepdims=True)
-        norm_t[at + 1 : at + 2, :] = jnp.sum(grad[...], axis=0, keepdims=True)
-    parts2[:, w2.shape[1] :] = norm_t[...].T.astype(low)
-    reduces[2].begin()
-    for at, ref in enumerate((branch, n1g, n2g)):
-        to_peer[at] = ref[theirs, :].astype(low)
-    sender.send(to_peer, from_peer, arrivals.at("y"), me, 1 - side, None, lambda: to_peer)
-    reduces[0].middle(2)
-    reduces[1].cores()
-    reduces[0].middle(1)
-    reduces[0].arrive()
-    reduces[1].middle(2)
-    reduces[2].cores()
-    reduces[1].middle(1)
-    reduces[1].arrive()
-    reduces[2].middle(2)
-    arrivals.wait(from_peer, "y")
-    tok_f = tok[...].astype(f32)
-    output[...] = (tok_f + (branch[mine, :] + from_peer[0].astype(f32))).astype(low)
-    one, two = (ref[mine, :] + from_peer[at].astype(f32) for at, ref in ((1, n1g), (2, n2g)))
-    hat, inverse = plain_norm(tok_f)
-    grad = one * params[0:1, :] + two * params[2:3, :]
-    grad_tokens[...] = cot[...].astype(f32) + inverse * (
-        grad
-        - jnp.mean(grad, axis=-1, keepdims=True)
-        - hat * jnp.mean(grad * hat, axis=-1, keepdims=True)
-    )
-    reduces[2].middle(1)
-    reduces[2].arrive()
-    norm_send[...] = total2[:, w2.shape[1] :]
-    sender.send(norm_send, norm_recv, arrivals.at("n"), me, 1 - side, None, lambda: norm_send)
-    arrivals.wait(norm_recv, "n")
-    total2[:, w2.shape[1] :] = norm_send[...] + norm_recv[...]
+    def norm_sums():
+        for at, grad in ((0, n1g), (2, n2g)):
+            norm_t[at : at + 1, :] = jnp.sum(grad[...] * xhat[...], axis=0, keepdims=True)
+            norm_t[at + 1 : at + 2, :] = jnp.sum(grad[...], axis=0, keepdims=True)
+        parts1[:, w1.shape[1] :] = norm_t[...].T.astype(low)
+
+    def rows_sent():
+        for at, ref in enumerate((branch, n1g, n2g)):
+            to_peer[at] = ref[theirs, :].astype(low)
+        sender.send(to_peer, from_peer, arrivals.at("y"), me, 1 - side, None, lambda: to_peer)
+
+    def rows_out():
+        arrivals.wait(from_peer, "y")
+        tok_f = tok[...].astype(f32)
+        output[...] = (tok_f + (branch[mine, :] + from_peer[0].astype(f32))).astype(low)
+        one, two = (ref[mine, :] + from_peer[at].astype(f32) for at, ref in ((1, n1g), (2, n2g)))
+        hat, inverse = plain_norm(tok_f)
+        grad = one * params[0:1, :] + two * params[2:3, :]
+        grad_tokens[...] = cot[...].astype(f32) + inverse * (
+            grad
+            - jnp.mean(grad, axis=-1, keepdims=True)
+            - hat * jnp.mean(grad * hat, axis=-1, keepdims=True)
+        )
+
+    def norms_out():
+        norm_send[...] = total1[:, w1.shape[1] :]
+        sender.send(norm_send, norm_recv, arrivals.at("n"), me, 1 - side, None, lambda: norm_send)
+        arrivals.wait(norm_recv, "n")
+        total1[:, w1.shape[1] :] = norm_send[...] + norm_recv[...]
+
+    steps = {
+        "ts": tokens_sent, "th": tokens_here, "na": norms_applied, "pr": projections,
+        "ag": attention_grads, "ab": attention_back, "ns": norm_sums, "rs": rows_sent,
+        "ro": rows_out, "no": norms_out,
+        "h1": lambda: hidden_part(w1, parts1),
+    }
+    for j in range(wide // 128):
+        steps[f"p{j}"] = functools.partial(pair, j)
+    for i, item in enumerate(gathers):
+        steps[f"g{i}b"], steps[f"g{i}f"] = item.begin, item.finish
+        for near in (1, 2, 3):
+            steps[f"g{i}{near}"] = functools.partial(item.hop, near)
+    for i, item in enumerate(reduces):
+        steps[f"r{i}b"], steps[f"r{i}c"], steps[f"r{i}a"] = item.begin, item.cores, item.arrive
+        for far in (2, 1):
+            steps[f"r{i}{far}"] = functools.partial(item.middle, far)
+    greet(z, x, core, side)
+    for line in ORDER:
+        for name in line.split():
+            steps[name]()
     sender.drain()
 
 
@@ -797,7 +806,7 @@
     low, f32 = jnp.bfloat16, jnp.float32
     vmem = pl.BlockSpec(memory_space=pltpu.VMEM)
     wide = heads * HEAD
-    widths = [4 * wide, shards[1].shape[1], shards[2].shape[1] + 128]
+    widths = [4 * wide, shards[1].shape[1] + 128]
     out_shape = [jax.ShapeDtypeStruct(tok.shape, low), jax.ShapeDtypeStruct(tok.shape, f32)]
     out_shape += [jax.ShapeDtypeStruct((48, w), f32) for w in widths]
     scratch = [pltpu.VMEM((d, s.shape[1]), low) for s in shards]
@@ -819,14 +828,14 @@
     return pl.pallas_call(
         layer_kernel,
         out_shape=out_shape,
-        in_specs=[vmem] * 9,
-        out_specs=[vmem] * 5,
+        in_specs=[vmem] * 6,
+        out_specs=[vmem] * 4,
         scratch_shapes=scratch,
         compiler_params=pltpu.CompilerParams(
             collective_id=0, has_side_effects=True, vmem_limit_bytes=58 * 1024 * 1024
         ),
         name="layer",
-    )(*shards, tok, cot, *waves, open_mask)
+    )(*shards, tok, cot, waves, open_mask)
 
 
 def plain_norm(values):
@@ -842,14 +851,13 @@
     heads = w_qkv.shape[1] // (3 * HEAD)
     own = w_qkv.shape[0]
     wide = heads * HEAD
-    split = w_up.shape[1] // 2
+    split = w_up.shape[1]
     norm_params = jnp.stack([ln1_gain, ln1_bias, ln2_gain, ln2_bias], axis=1)
     qkv = w_qkv.reshape(own, heads, 3, HEAD).transpose(0, 2, 1, 3).reshape(own, 3 * wide)
     down = w_down.T
     shards = (
         jnp.concatenate([qkv, w_out.T, jnp.pad(norm_params, ((0, 0), (0, 124)))], axis=1),
-        jnp.concatenate([w_up[:, :split], down[:, :split]], axis=1),
-        jnp.concatenate([w_up[:, split:], down[:, split:]], axis=1),
+        jnp.concatenate([w_up, down], axis=1),
     )
     rows = 2 * tokens.shape[0]
     segment, positions, places = doc_layout(lengths[0], rows)
@@ -860,13 +868,13 @@
     blank = jnp.zeros((rows, rest), jnp.float32)
     sin_low = jnp.concatenate([wave_sin, none, blank], axis=1)
     sin_high = jnp.concatenate([none, wave_sin, blank], axis=1)
-    waves = [jnp.concatenate([table, table], axis=1) for table in (cos, sin_low, sin_high)]
+    waves = jnp.concatenate([cos, cos, sin_low, sin_low, sin_high, sin_high], axis=1)
     allowed = (segment[:, None] == segment[None, :]) & (places[:, None] >= places[None, :])
-    output, grad_tokens, total0, total1, total2 = layer_call(
+    output, grad_tokens, total0, total1 = layer_call(
         shards, tokens, grad_out, waves, allowed.astype(jnp.float32), heads
     )
     qkv_grad = total0[:, : 3 * wide].reshape(own, 3, heads, HEAD).transpose(0, 2, 1, 3)
-    norm_total = total2[:, 2 * split : 2 * split + 4].T
+    norm_total = total1[:, 2 * split : 2 * split + 4].T
     return (
         output,
         grad_tokens,
@@ -876,8 +884,8 @@
         norm_total[3],
         qkv_grad.reshape(own, 3 * wide),
         total0[:, 3 * wide :].T,
-        jnp.concatenate([total1[:, :split], total2[:, :split]], axis=1),
-        jnp.concatenate([total1[:, split:], total2[:, split : 2 * split]], axis=1).T,
+        total1[:, :split],
+        total1[:, split : 2 * split].T,
     )
 
 

time: 142 us -> 135 us (0.951); the launches traced: 139 us -> 133 us
  Pallas kernels: 121 us -> 118 us
  other arithmetic: 4.59 us -> 3.13 us
    pallas_call x1, Pallas kernels: 121 us -> 118 us  [layer_call(): pl.pallas_call(layer_kernel, out_shape=out_shape, in_specs=[vmem] * 6, ou...]
    slice x4 -> x0, local copies, waits for them, and re-layouts: 2.05 us -> none  [the longest x1 1.05 us: line_device(): total2[:, split:2 * split]]
    transpose x1 -> x2, local copies, waits for them, and re-layouts: 0.74 us -> 2.69 us  [the longest x1 1.94 us: line_device(): total1[:, split:2 * split]]
where the time goes in v3:
time: 135 us; the launch traced here: 133 us
  Pallas kernels  118 us (87%)
  local copies, waits for them, and re-layouts  11.6 us (9%)
  other arithmetic  3.13 us (2%)
    pallas_call x1, Pallas kernels, layer_call(): pl.pallas_call(layer_kernel, out_shape=out_shape, in_specs=[vmem] * 6, ou...  118 us
    unnamed x26, local copies, waits for them, and re-layouts  4.13 us

profile of v3, /device:TPU:8, one launch (start us, length us, event | category | flops | bytes accessed | tf_op | source)
XLA Modules:
  0.0 133.3 jit_solution(2866323249441993410)
XLA Ops:
  0.6 0.0 copy-start.11
  0.7 0.6 copy-done.11
  1.3 0.2 reduce-window.4
  1.5 0.1 convert_reduce_fusion
  1.6 0.1 select_reduce_fusion
  1.7 0.0 copy-start.7
  1.7 0.0 copy-start.8
  1.7 0.0 copy-start.9
  1.7 0.0 copy-start.10
  1.7 0.6 copy-done.7
  2.3 0.0 copy-done.8
  2.3 0.0 copy-done.9
  2.4 0.0 copy-done.10
  2.4 0.1 copy.40
  2.5 0.5 multiply_sine_fusion
  3.1 1.5 %concatenate.15.refs_4_ = f32[256,384]{1,0:T(8,128)} concatenate(f32[256,8]{1,0:T(8,128)S(1)} %get-tuple-element.25, f32[256,8]{1,0:T(8,128)S(1)} %get-tuple-element.25, f32[256,48]{1,0:T(8,128)S(1)} %broadcast_in_dim.37, f32[256,8]{1,0:T(8,128)S(1)} %get-tuple-element.25, f32[256,8]{1,0:T(8,128)S(1)} %get-tuple-element.25, f32[256,48]{1,0:T(8,128)S(1)} %broadcast_in_dim.37, ...), dimensions={1} | concatenate | bytes 786432 | tf_op jit(solution)/shard_map/concatenate | solution.py:871
  4.6 0.0 copy-start.5
  4.6 0.8 fusion.2.refs_5_
  5.4 0.1 copy-done.5
  5.5 0.2 reshape.56
  5.7 0.1 copy.39
  5.8 0.0 copy-start.6
  5.8 0.2 reshape.57
  6.0 0.5 copy-done.6
  6.5 0.0 copy-start.3
  6.5 0.0 copy-start.4
  6.5 0.7 fusion.3.refs_0_
  7.2 0.3 copy-done.3
  7.5 0.1 copy-done.4
  7.6 0.7 pad_maximum_fusion.refs_1_
  8.3 117.8 %layer.1 = (bf16[128,768]{1,0:T(8,128)(2,1)}, f32[128,768]{1,0:T(8,128)}, f32[48,1536]{1,0:T(8,128)}, f32[48,3200]{1,0:T(8,128)}) custom-call(bf16[48,1664]{1,0:T(8,128)(2,1)} %fusion.3.refs_0_, bf16[48,3072]{1,0:T(8,128)(2,1)} %pad_maximum_fusion.refs_1_, bf16[128,768]{1,0:T(8,128)(2,1)} %refs_2_.1, bf16[128,768]{1,0:T(8,128)(2,1)} %refs_3_.1, ...), custom_call_target="tpu_custom_call" | custom-call | tf_op jit(solution)/shard_map/layer/pallas_call | solution.py:828
  126.1 0.7 slice_bitcast_fusion.2
  126.9 0.0 copy-start.1
  126.9 1.9 %slice_bitcast_fusion = (f32[1536,48]{0,1:T(8,128)}, f32[48,1536]{1,0:T(8,128)}) fusion(f32[48,3200]{1,0:T(8,128)} %get-tuple-element.16), kind=kLoop, calls=%fused_computation.3 | loop fusion | bytes 1179648 | tf_op jit(solution)/shard_map/transpose | solution.py:888
  128.8 0.7 slice_reduce_fusion
  129.6 0.0 copy-done.1
  129.6 0.6 slice_bitcast_fusion.1
  130.2 0.1 reshape.60
  130.4 0.2 copy.42
  130.5 0.0 copy-start.2
  130.5 1.0 reshape.61
  131.5 0.0 copy-done.2
  131.5 0.0 copy-start
  131.5 0.7 copy.45
  132.2 0.4 copy-done
  132.6 0.7 copy.46
  (8 shorter events, 0.1 us)
Async XLA Ops:
  0.6 0.7 copy-start.11
  1.7 0.7 copy-start.7
  1.7 0.7 copy-start.8
  1.7 0.7 copy-start.9
  1.7 0.7 copy-start.10
  4.6 0.9 copy-start.5
  5.8 0.8 copy-start.6
  6.5 1.0 copy-start.3
  6.5 1.0 copy-start.4
  126.9 2.7 %copy-start.1 = (f32[48,1536]{1,0:T(8,128)S(1)}, f32[48,1536]{1,0:T(8,128)}, u32[]{:S(2)}) copy-start(f32[48,1536]{1,0:T(8,128)} %get-tuple-element.17) | copy-start | bytes 884740
  130.5 1.0 copy-start.2
  131.5 1.1 copy-start
